TPU v7x, 512 devices: a whole 4x8x8 slice. The times are simulated.
512 devices in a mesh: row: 8 (over y_lo, x), col: 8 (over y_hi, core), depth: 8 (over z).
Axes of the slice: x: 4, y: 8 (y_hi: 4, y_lo: 2; y = y_hi * 2 + y_lo), z: 8, core: 2. Of those that a mesh axis runs over, the one named last changes fastest.
Arguments:
- residual: bfloat16 [1024, 4096], P(('row', 'depth'), 'col'), may hold values from -48 to 48
- pre_gain: float32 [4096], P('col'), may hold values from 0.1 to 1.9
- w_gate: bfloat16 [4096, 16384], P('row', ('col', 'depth')), may hold values from -0.09375 to 0.09375
- w_up: bfloat16 [4096, 16384], P('row', ('col', 'depth')), may hold values from -0.09375 to 0.09375
- w_down: bfloat16 [16384, 4096], P(('col', 'depth'), 'row'), may hold values from -0.125 to 0.125
- value_head: float32 [4096], P('col'), may hold values from -0.0234375 to 0.0234375
- sample_index: int32 [1024], P(('row', 'depth')), may hold values from 0 to 32767
- return_table: float32 [32768], replicated, may hold values from -6 to 6
Outputs:
- values: float32 [1024], P(('row', 'depth'))
- grad_gate_weight: bfloat16 [4096, 16384], P('row', ('col', 'depth'))
- grad_up_weight: bfloat16 [4096, 16384], P('row', ('col', 'depth'))
- grad_down_weight: bfloat16 [16384, 4096], P(('col', 'depth'), 'row')
- grad_value: float32 [4096], P('col')
All inputs are finite; a program needn't handle non-finite values.
Results may differ from a plain program's by a relative error of at most 0.013.
Values may be sent and summed in bfloat16 or wider, within the bound.
A program may use at most 64 MiB of HBM per device.

v0:
```python
import jax
import jax.numpy as jnp
from jax import lax
from jax.sharding import PartitionSpec as P

D = 4096


norm_eps = 1e-06
huber_delta = 1.0


def contract_rows(left, right):
    return lax.dot_general(
        left, right, (((0,), (0,)), ((), ())), preferred_element_type=jnp.float32
    )


def contract_columns(left, right):
    return lax.dot_general(
        left, right, (((1,), (1,)), ((), ())), preferred_element_type=jnp.float32
    )


def per_device(residual, pre_gain, w_gate, w_up, w_down, value_head, sample_index, return_table):
    wide = residual.astype(jnp.float32)
    squares = lax.psum(jnp.sum(wide * wide, axis=1), "col")
    inv_norm = lax.rsqrt(squares / D + norm_eps)
    normed = (wide * inv_norm[:, None] * pre_gain[None, :]).astype(jnp.bfloat16)
    normed_slices = lax.all_to_all(normed, "depth", split_axis=1, concat_axis=0, tiled=True)
    normed_panel = lax.all_gather(normed_slices, ("col", "depth"), axis=1, tiled=True)
    normed_rows = lax.all_to_all(normed_panel, "row", split_axis=1, concat_axis=0, tiled=True)
    pieces = (
        lax.all_gather(w_gate, "row", axis=0, tiled=True),
        lax.all_gather(w_up, "row", axis=0, tiled=True),
    )
    columns = normed_panel
    gate_value = jnp.dot(columns, pieces[0], preferred_element_type=jnp.float32)
    up_value = jnp.dot(columns, pieces[1], preferred_element_type=jnp.float32)
    sigmoid_gate = jax.nn.sigmoid(gate_value)
    hidden = (gate_value * sigmoid_gate * up_value).astype(jnp.bfloat16)
    partial_value = jnp.dot(
        hidden,
        lax.all_gather(w_down, "row", axis=1, tiled=True),
        preferred_element_type=jnp.float32,
    )
    summed = lax.psum_scatter(partial_value, ("col", "depth"), scatter_dimension=1, tiled=True)
    output = (
        lax.all_to_all(
            summed.astype(jnp.bfloat16), "depth", split_axis=0, concat_axis=1, tiled=True
        ).astype(summed.dtype)
        + wide
    )
    out_squares = lax.psum(jnp.sum(output * output, axis=1), "col")
    inv_final = lax.rsqrt(out_squares / D + norm_eps)
    final = output * inv_final[:, None]
    values = lax.psum(jnp.sum(final * value_head[None, :], axis=1), "col")
    target = jnp.take(return_table, sample_index)
    slope = jnp.clip(values - target, -huber_delta, huber_delta)
    grad_value = lax.psum(jnp.sum(final * slope[:, None], axis=0), ("row", "depth"))
    inner = slope * values / D
    grad_output = (
        inv_final[:, None] * (slope[:, None] * value_head[None, :] - final * inner[:, None])
    ).astype(jnp.bfloat16)
    grad_slices = lax.all_to_all(grad_output, "depth", split_axis=1, concat_axis=0, tiled=True)
    grad_panel = lax.all_gather(grad_slices, ("col", "depth"), axis=1, tiled=True)
    grad_rows = lax.all_to_all(grad_panel, "row", split_axis=1, concat_axis=0, tiled=True)
    columns = grad_panel
    grad_hidden = contract_columns(columns, lax.all_gather(w_down, "row", axis=1, tiled=True))
    grad_gate = (
        grad_hidden * up_value * sigmoid_gate * (1.0 + gate_value * (1.0 - sigmoid_gate))
    ).astype(jnp.bfloat16)
    grad_up = (grad_hidden * gate_value * sigmoid_gate).astype(jnp.bfloat16)
    block = grad_rows
    grad_down_weight = contract_rows(
        lax.all_gather(hidden, "row", axis=0, tiled=True), block
    ).astype(jnp.bfloat16)
    pieces = (
        lax.all_gather(grad_gate, "row", axis=0, tiled=True),
        lax.all_gather(grad_up, "row", axis=0, tiled=True),
    )
    block = normed_rows
    grad_gate_weight = contract_rows(block, pieces[0])
    grad_up_weight = contract_rows(block, pieces[1])
    return (
        values,
        grad_gate_weight.astype(jnp.bfloat16),
        grad_up_weight.astype(jnp.bfloat16),
        grad_down_weight,
        grad_value,
    )


def solution(mesh):
    placed = (
        P(("row", "depth"), "col"),
        P("col"),
        P("row", ("col", "depth")),
        P("row", ("col", "depth")),
        P(("col", "depth"), "row"),
        P("col"),
        P(("row", "depth")),
        P(),
    )
    return jax.shard_map(
        per_device,
        mesh=mesh,
        in_specs=placed,
        out_specs=(
            P(("row", "depth")),
            P("row", ("col", "depth")),
            P("row", ("col", "depth")),
            P(("col", "depth"), "row"),
            P("col"),
        ),
        check_vma=False,
    )
```

profile of v0, /device:TPU:16, one launch (start us, length us, event | category | flops | bytes accessed | tf_op | source)
XLA Modules:
  0.0 823.3 jit_solution(2157603795203044623)
XLA Ops:
  8.1 15.6 %psum.28 = f32[16]{0:T(128)S(1)} all-reduce(f32[16]{0:T(128)S(1)} %fusion), channel_id=1, replica_groups=mesh['row'=8,'col'=8,'depth'=8] {'col'}, use_global_device_ids=true, to_apply=%region_1.0 | all-reduce | flops 16 | bytes 128 | tf_op jit(solution)/shard_map/psum | solution.py:27
  24.7 16.2 %all_to_all.89 = bf16[8,2,512]{2,1,0:T(2,128)(2,1)S(1)} all-to-all(bf16[8,2,512]{2,1,0:T(2,128)(2,1)S(1)} %reshape.48), channel_id=1, replica_groups=mesh['row'=8,'col'=8,'depth'=8] {'depth'}, dimensions={0} | all-to-all | bytes 32768 | tf_op jit(solution)/shard_map/all_to_all | solution.py:30
  43.8 77.3 %all-gather.6.cloned.1.call-done = bf16[128,4096]{0,1:T(8,128)(2,1)} async-done(((bf16[128,64]{0,1:T(8,128)(2,1)}), bf16[128,4096]{0,1:T(8,128)(2,1)}) %all-gather.6.cloned.1.call-update) | async-done | bytes 1048592 | tf_op jit(solution)/shard_map/all_gather | solution.py:31
  121.1 45.2 %all-gather.8.cloned.1.call-done = bf16[4096,256]{1,0:T(8,128)(2,1)} async-done(((bf16[512,256]{1,0:T(8,128)(2,1)}), bf16[4096,256]{1,0:T(8,128)(2,1)}) %all-gather.8.cloned.1.call-update) | async-done | bytes 2097168 | tf_op jit(solution)/shard_map/all_gather | solution.py:34
  166.3 2.4 fusion.6
  168.7 45.8 %all-gather.10.cloned.1.call-done = bf16[4096,256]{1,0:T(8,128)(2,1)} async-done(((bf16[512,256]{1,0:T(8,128)(2,1)}), bf16[4096,256]{1,0:T(8,128)(2,1)}) %all-gather.10.cloned.1.call-update) | async-done | bytes 2097168 | tf_op jit(solution)/shard_map/all_gather | solution.py:35
  214.6 2.8 multiply_convert_fusion.2
  217.3 45.7 %all-gather.12.cloned.1.call-done = bf16[256,4096]{1,0:T(8,128)(2,1)} async-done(((bf16[256,512]{1,0:T(8,128)(2,1)}), bf16[256,4096]{1,0:T(8,128)(2,1)}) %all-gather.12.cloned.1.call-update) | async-done | bytes 2097168 | tf_op jit(solution)/shard_map/all_gather | solution.py:44
  263.1 3.9 fusion.7
  267.6 150.2 %reduce-scatter.2.cloned.1.call-done = f32[128,64]{0,1:T(8,128)} async-done(((f32[128,4096]{0,1:T(8,128)}), f32[128,64]{0,1:T(8,128)}) %reduce-scatter.2.cloned.1.call-update) | async-done | bytes 32784 | tf_op jit(solution)/shard_map/reduce_scatter | solution.py:47
  419.3 5.4 all-to-all-start.1
  425.5 7.1 all-to-all-done.1
  432.9 11.8 %psum.29 = f32[16]{0:T(128)S(1)} all-reduce(f32[16]{0:T(128)S(1)} %multiply_reduce_fusion.2), channel_id=1, replica_groups=mesh['row'=8,'col'=8,'depth'=8] {'col'}, use_global_device_ids=true, to_apply=%region_4.0 | all-reduce | flops 16 | bytes 128 | tf_op jit(solution)/shard_map/psum | solution.py:54
  444.9 14.2 %psum.30 = f32[16]{0:T(128)S(1)} all-reduce(f32[16]{0:T(128)S(1)} %multiply_reduce_fusion.1), channel_id=1, replica_groups=mesh['row'=8,'col'=8,'depth'=8] {'col'}, use_global_device_ids=true, to_apply=%region_6.0 | all-reduce | flops 16 | bytes 128 | tf_op jit(solution)/shard_map/psum | solution.py:57
  459.4 10.1 %all_to_all.90 = bf16[8,2,512]{2,1,0:T(2,128)(2,1)S(1)} all-to-all(bf16[8,2,512]{2,1,0:T(2,128)(2,1)S(1)} %reshape.52), channel_id=1, replica_groups=mesh['row'=8,'col'=8,'depth'=8] {'depth'}, dimensions={0} | all-to-all | bytes 32768 | tf_op jit(solution)/shard_map/all_to_all | solution.py:65
  470.3 18.6 %all_to_all.91 = bf16[128,8,512]{0,2,1:T(8,128)(2,1)} all-to-all(bf16[128,8,512]{0,2,1:T(8,128)(2,1)S(1)} %bitcast.37), channel_id=1, replica_groups=mesh['row'=8,'col'=8,'depth'=8] {'row'}, dimensions={1} | all-to-all | bytes 2097152 | tf_op jit(solution)/shard_map/all_to_all | solution.py:32
  488.9 60.3 %all-gather.14.cloned.1.call-done = bf16[128,4096]{0,1:T(8,128)(2,1)} async-done(((bf16[128,64]{0,1:T(8,128)(2,1)}), bf16[128,4096]{0,1:T(8,128)(2,1)}) %all-gather.14.cloned.1.call-update) | async-done | bytes 1048592 | tf_op jit(solution)/shard_map/all_gather | solution.py:66
  549.2 4.8 all-to-all-start.4
  554.1 41.5 %all_gather.32 = bf16[1024,256]{1,0:T(8,128)(2,1)} all-gather(bf16[128,256]{1,0:T(8,128)(2,1)S(1)} %get-tuple-element.11), channel_id=1, replica_groups=mesh['row'=8,'col'=8,'depth'=8] {'row'}, dimensions={0}, use_global_device_ids=true | all-gather | bytes 589824 | tf_op jit(solution)/shard_map/all_gather | solution.py:76
  595.6 2.3 copy.35
  597.9 154.9 %psum.31 = f32[512]{0:T(512)} all-reduce(f32[512]{0:T(512)S(1)} %get-tuple-element.9), channel_id=1, replica_groups=mesh['row'=8,'col'=8,'depth'=8] {'row','depth'}, use_global_device_ids=true, to_apply=%region_8.9 | all-reduce | flops 512 | bytes 4096 | tf_op jit(solution)/shard_map/psum | solution.py:60
  753.7 28.9 %all_gather.31 = bf16[1024,256]{1,0:T(8,128)(2,1)S(1)} all-gather(bf16[128,256]{1,0:T(8,128)(2,1)S(1)} %get-tuple-element.7), channel_id=1, replica_groups=mesh['row'=8,'col'=8,'depth'=8] {'row'}, dimensions={0}, use_global_device_ids=true | all-gather | bytes 589824 | tf_op jit(solution)/shard_map/all_gather | solution.py:80
  782.6 28.8 %all_gather.30 = bf16[1024,256]{1,0:T(8,128)(2,1)S(1)} all-gather(bf16[128,256]{1,0:T(8,128)(2,1)S(1)} %get-tuple-element.8), channel_id=1, replica_groups=mesh['row'=8,'col'=8,'depth'=8] {'row'}, dimensions={0}, use_global_device_ids=true | all-gather | bytes 589824 | tf_op jit(solution)/shard_map/all_gather | solution.py:79
  813.8 1.5 copy.38
  (67 shorter events, 13.7 us)
Async XLA Ops:
  7.2 417.6 %copy-start = (f32[32768]{0:T(1024)S(1)}, f32[32768]{0:T(1024)}, u32[]{:S(2)}) copy-start(f32[32768]{0:T(1024)} %param.15) | copy-start | bytes 393220
  7.2 113.9 %all-gather.6.cloned.1.call-start = ((), (), s32[]{:S(2)}) async-start(), calls=%async_computation.6 | async-start | bytes 1064960 | tf_op jit(solution)/shard_map/all_gather | solution.py:31
  41.7 124.6 %all-gather.8.cloned.1.call-start = ((), (), s32[]{:S(2)}) async-start(), calls=%async_computation.7 | async-start | bytes 2359296 | tf_op jit(solution)/shard_map/all_gather | solution.py:34
  42.4 172.1 %all-gather.10.cloned.1.call-start = ((), (), s32[]{:S(2)}) async-start(), calls=%async_computation.8 | async-start | bytes 2359296 | tf_op jit(solution)/shard_map/all_gather | solution.py:35
  43.2 219.9 %all-gather.12.cloned.1.call-start = ((), (), s32[]{:S(2)}) async-start(), calls=%async_computation.9 | async-start | bytes 2359296 | tf_op jit(solution)/shard_map/all_gather | solution.py:44
  43.7 374.0 %reduce-scatter.2.cloned.1.call-start = ((), (), s32[]{:S(2)}) async-start(), calls=%async_computation.10 | async-start | bytes 2129920 | tf_op jit(solution)/shard_map/reduce_scatter | solution.py:47
  121.1 93.5 %copy-start.1 = (bf16[128,4096]{0,1:T(8,128)(2,1)S(1)}, bf16[128,4096]{0,1:T(8,128)(2,1)}, u32[]{:S(2)}) copy-start(bf16[128,4096]{0,1:T(8,128)(2,1)} %all-gather.6.cloned.1.call-done) | copy-start | bytes 3145732
  266.9 0.7 copy-start.9
  266.9 165.8 %copy-start.7 = (bf16[16,512]{1,0:T(8,128)(2,1)S(1)}, bf16[16,512]{1,0:T(8,128)(2,1)}, u32[]{:S(2)}) copy-start(bf16[16,512]{1,0:T(8,128)(2,1)} %param.8) | copy-start | bytes 49156
  266.9 177.7 %copy-start.8 = (f32[512]{0:T(512)S(1)}, f32[512]{0:T(512)}, u32[]{:S(2)}) copy-start(f32[512]{0:T(512)} %param.13) | copy-start | bytes 6148
  419.3 13.2 %all-to-all-start.1 = ((bf16[8,2,512]{2,1,0:T(2,128)(2,1)}), bf16[8,2,512]{2,1,0:T(2,128)(2,1)S(1)}, u32[]{:S(2)}, u32[]{:S(2)}) async-start(bf16[8,2,512]{2,1,0:T(2,128)(2,1)} %reshape.50), calls=%async_computation.2 | async-start | bytes 32768 | tf_op jit(solution)/shard_map/all_to_all | solution.py:49
  424.7 124.5 %all-gather.14.cloned.1.call-start = ((), (), s32[]{:S(2)}) async-start(), calls=%async_computation.11 | async-start | bytes 1064960 | tf_op jit(solution)/shard_map/all_gather | solution.py:66
  459.1 90.2 %copy-start.10 = (f32[16]{0:T(128)}, f32[16]{0:T(128)S(1)}, u32[]{:S(2)}) copy-start(f32[16]{0:T(128)S(1)} %psum.30) | copy-start | bytes 196
  549.2 203.6 %copy-start.2 = (bf16[256,4096]{1,0:T(8,128)(2,1)S(1)}, bf16[256,4096]{1,0:T(8,128)(2,1)}, u32[]{:S(2)}) copy-start(bf16[256,4096]{1,0:T(8,128)(2,1)} %all-gather.12.cloned.1.call-done) | copy-start | bytes 6291460
  549.2 203.6 %copy-start.3 = (bf16[128,4096]{0,1:T(8,128)(2,1)S(1)}, bf16[128,4096]{0,1:T(8,128)(2,1)}, u32[]{:S(2)}) copy-start(bf16[128,4096]{0,1:T(8,128)(2,1)} %all-gather.14.cloned.1.call-done) | copy-start | bytes 3145732
  549.2 264.5 %all-to-all-start.4 = ((bf16[128,8,512]{0,2,1:T(8,128)(2,1)}), bf16[128,8,512]{0,2,1:T(8,128)(2,1)}, u32[]{:S(2)}, u32[]{:S(2)}) async-start(bf16[128,8,512]{0,2,1:T(8,128)(2,1)} %bitcast.38), calls=%async_computation.5 | async-start | bytes 2097152 | tf_op jit(solution)/shard_map/all_to_all | solution.py:67
  595.6 157.2 %copy-start.5 = (f32[128,256]{1,0:T(8,128)S(1)}, f32[128,256]{1,0:T(8,128)}, u32[]{:S(2)}) copy-start(f32[128,256]{1,0:T(8,128)} %get-tuple-element.12) | copy-start | bytes 393220
  752.8 58.6 %copy-start.4 = (bf16[8,128,512]{2,1,0:T(8,128)(2,1)S(1)}, bf16[8,128,512]{2,1,0:T(8,128)(2,1)}, u32[]{:S(2)}) copy-start(bf16[8,128,512]{2,1,0:T(8,128)(2,1)} %copy.35) | copy-start | bytes 3145732
  812.6 2.7 copy-start.6
Sparse Core Ops, SparseCore 0:
  41.8 79.2 all-gather.5
  123.2 43.0 all-gather.7
  168.4 46.1 all-gather.9
  216.5 46.5 all-gather.11
  267.5 150.1 reduce-scatter.1
  470.4 78.7 all-gather.13
where the time goes:
time: 824 us; the launch traced here: 823 us
  waiting for transfers between devices  434 us (53%)
  blocking collectives  341 us (41%)
  between operations  14.2 us (2%)
  matrix products  13.4 us (2%)
  starting transfers between devices  10.5 us (1%)
    psum x1, blocking collectives, per_device(): lax.psum(jnp.sum(final * slope[:, None], axis=0), ('row', 'depth'))  155 us
    reduce_scatter x1, waiting for transfers between devices, per_device(): lax.psum_scatter(partial_value, ('col', 'depth'), scatter_dimension=1, ti...  150 us
    all_gather x1, waiting for transfers between devices, per_device(): lax.all_gather(normed_slices, ('col', 'depth'), axis=1, tiled=True)  77.3 us
    all_gather x1, waiting for transfers between devices, per_device(): lax.all_gather(grad_slices, ('col', 'depth'), axis=1, tiled=True)  60.3 us
    all_gather x1, waiting for transfers between devices, per_device(): lax.all_gather(w_up, 'row', axis=0, tiled=True)  45.8 us
    all_gather x1, waiting for transfers between devices, per_device(): lax.all_gather(w_down, 'row', axis=1, tiled=True)  45.7 us
    all_gather x1, waiting for transfers between devices, per_device(): lax.all_gather(w_gate, 'row', axis=0, tiled=True)  45.2 us
    all_gather x1, blocking collectives, per_device(): lax.all_gather(hidden, 'row', axis=0, tiled=True)  41.5 us
  transfers between devices with their start and end apart: 8, of which 7 were waited for; matrix products, arithmetic and copies ran while one was open for 1% of the time, Pallas kernels for 0%

commit v1 on v0

v1 whole, which is shorter than its diff:
```python
import functools

import jax
import jax.numpy as jnp
from jax import lax
from jax.experimental import pallas as pl
from jax.experimental.pallas import tpu as pltpu
from jax.sharding import PartitionSpec as P

MESH = pl.DeviceIdType.MESH
norm_eps = 1e-06
huber_delta = 1.0


def rem(value, size):
    return lax.rem(value, jnp.int32(size))


def dot(left, right):
    return jnp.dot(left, right, preferred_element_type=jnp.float32)


def kernel(
    R, YH, Z, B, F, H,
    x_ref, gv_ref, tgt_ref, wg_ref, wu_ref, wd_ref,
    dg_ref, du_ref, dd_ref, val_ref, gval_ref,
    xbuf, ybuf, ytbuf, rssend, rsrecv, guown, st1send, st1recv,
    hbuf, htbuf, gatebuf, upbuf, invbuf,
    osend, osib, oown, zsend, zrecv, ysend, yrecv, obuf,
    st2send, st2recv, abuf, bbuf, gobuf, ghsend, ghrecv, ghown, ggbuf,
    gvbuf, gvsend, gvrecv, tg1, tg2send, tg2,
    s1_s, s1_r, gv_s, gv_r, t1_s, t1_r, t2_s, t2_r,
    z1_s, z1_r, b1_s, b1_r, rs_s, rs_r, q1_s, q1_r, h_s, h_r,
    ob_s, ob_r, oz_s, oz_r, oy_s, oy_r, ay_s, ay_r, az_s, az_r, ab_s, ab_r,
    q2_s, q2_r, gh_s, gh_r, gg_s, gg_r, go_s, go_r,
):
    r = lax.axis_index("row")
    c = lax.axis_index("col")
    d = lax.axis_index("depth")
    core = rem(c, 2)
    yh = lax.div(c, jnp.int32(2))
    rpar = rem(r, 2)
    rj = lax.div(r, jnp.int32(2))
    T = 2 * YH * B
    half = YH * B
    features = R * F
    diagonal = r == c

    def copy(src, dst, send, recv, device):
        return pltpu.make_async_remote_copy(
            src_ref=src, dst_ref=dst, send_sem=send, recv_sem=recv,
            device_id=device, device_id_type=MESH,
        )

    def row_peer(k):
        return rem(r + k, R)

    def depth_peer(k):
        return rem(d + k, Z)

    def y_peer(k):
        return rem(yh + k, YH)

    def row_device(q):
        return (q, c, d)

    def depth_device(q):
        return (r, c, q)

    def y_device(j):
        return (r, 2 * j + core, d)

    sibling = (r, 2 * yh + 1 - core, d)
    partner = (c, r, d)
    mine = pl.ds(pl.multiple_of(core * half, 16), half)
    other = pl.ds(pl.multiple_of((1 - core) * half, 16), half)

    def slot(parity, j):
        return pl.ds(pl.multiple_of(parity * half + j * B, 16), B)

    def loop(count, body, start=0):
        def step(k, carry):
            body(k)
            return carry
        lax.fori_loop(start, count, step, 0)

    eye = (
        lax.broadcasted_iota(jnp.int32, (T, T), 0)
        == lax.broadcasted_iota(jnp.int32, (T, T), 1)
    )

    def to_lanes(column):
        return jnp.sum(jnp.where(eye, column, 0.0), axis=0, keepdims=True)

    def to_column(lanes):
        return jnp.sum(jnp.where(eye, lanes, 0.0), axis=1, keepdims=True)

    barrier = pltpu.get_barrier_semaphore()

    def greet(device):
        pl.semaphore_signal(barrier, inc=1, device_id=device, device_id_type=MESH)

    for k in range(1, R):
        greet(row_device(row_peer(k)))
    for k in range(1, Z):
        greet(depth_device(depth_peer(k)))
    for k in range(1, YH):
        greet(y_device(y_peer(k)))
    greet(sibling)
    for j in range(YH):
        @pl.when(jnp.logical_not(diagonal & (yh == j)))
        def _():
            greet((2 * j + core, r, d))
    pl.semaphore_wait(
        barrier, (R - 1) + (Z - 1) + (YH - 1) + 1 + YH - jnp.where(diagonal, 1, 0)
    )

    def first_copy(j):
        return copy(
            x_ref, xbuf.at[d, slot(rpar, rj)], s1_s.at[j], s1_r.at[rj],
            (c, 2 * j + rpar, d),
        )

    def first_arrival(j):
        return copy(
            x_ref, xbuf.at[d, slot(core, j)], s1_s.at[j], s1_r.at[j],
            (2 * j + core, r, d),
        )

    for j in range(YH):
        local = diagonal & (yh == j)

        @pl.when(local)
        def _():
            xbuf[d, slot(core, j)] = x_ref[...]

        @pl.when(jnp.logical_not(local))
        def _():
            first_copy(j).start()

    gv_copy = copy(gv_ref, gvbuf, gv_s, gv_r, partner)

    @pl.when(diagonal)
    def _():
        gvbuf[...] = gv_ref[...]

    @pl.when(jnp.logical_not(diagonal))
    def _():
        gv_copy.start()

    def t1_copy(k):
        return copy(tgt_ref, tg1.at[r], t1_s.at[k], t1_r.at[k], row_device(row_peer(k)))

    def t1_arrival(k):
        q = row_peer(R - k)
        return copy(tgt_ref, tg1.at[q], t1_s.at[k], t1_r.at[k], row_device(q))

    for k in range(1, R):
        t1_copy(k).start()

    for j in range(YH):
        @pl.when(jnp.logical_not(diagonal & (yh == j)))
        def _():
            first_arrival(j).wait_recv()

    def gather_over_depth(buf, zs, zr, bs, br):
        def z_copy(k):
            return copy(
                buf.at[d, mine], buf.at[d, mine], zs.at[k], zr.at[k],
                depth_device(depth_peer(k)),
            )

        def z_arrival(k):
            q = depth_peer(Z - k)
            return copy(
                buf.at[q, mine], buf.at[q, mine], zs.at[k], zr.at[k], depth_device(q)
            )

        def s_copy(k):
            q = depth_peer(Z - k)
            return copy(buf.at[q, mine], buf.at[q, mine], bs.at[k], br.at[k], sibling)

        def s_arrival(k):
            q = depth_peer(Z - k)
            return copy(buf.at[q, other], buf.at[q, other], bs.at[k], br.at[k], sibling)

        return z_copy, z_arrival, s_copy, s_arrival

    near = []
    for k in range(1, Z // 2 + 1):
        near.append(k)
        if Z - k > k:
            near.append(Z - k)

    z_copy, z_arrival, s_copy, s_arrival = gather_over_depth(xbuf, z1_s, z1_r, b1_s, b1_r)
    for k in near:
        z_copy(k).start()
    s_copy(0).start()

    total = tgt_ref[...]
    for k in range(1, R):
        t1_arrival(k).wait_recv()
        total = total + tg1[row_peer(R - k)]
    tg2send[...] = total

    def t2_copy(k):
        return copy(tg2send, tg2.at[d], t2_s.at[k], t2_r.at[k], depth_device(depth_peer(k)))

    def t2_arrival(k):
        q = depth_peer(Z - k)
        return copy(tg2send, tg2.at[q], t2_s.at[k], t2_r.at[k], depth_device(q))

    for k in range(1, Z):
        t2_copy(k).start()

    for k in near:
        z_arrival(k).wait_recv()
        s_copy(k).start()

    @pl.when(jnp.logical_not(diagonal))
    def _():
        gv_copy.wait_recv()

    for k in range(Z):
        s_arrival(k).wait_recv()

    gain = gvbuf[0:1, :]

    def rs_copy(q):
        return copy(rssend.at[q], rsrecv.at[r], rs_s.at[q], rs_r.at[r], row_device(q))

    def rs_arrival(q):
        return copy(rssend.at[q], rsrecv.at[q], rs_s.at[q], rs_r.at[q], row_device(q))

    def q1_copy(q):
        return copy(st1send.at[q], st1recv.at[r], q1_s.at[q], q1_r.at[r], row_device(q))

    def q1_arrival(q):
        return copy(st1send.at[q], st1recv.at[q], q1_s.at[q], q1_r.at[q], row_device(q))

    def gate_up(q):
        wide = xbuf[q].astype(jnp.float32)
        squares = jnp.sum(wide * wide, axis=1, keepdims=True)
        st1send[q] = jnp.broadcast_to(to_lanes(squares), (8, T))
        scaled = (wide * gain).astype(jnp.bfloat16)
        ybuf[q] = scaled
        return dot(scaled, wg_ref[...]), dot(scaled, wu_ref[...])

    def gate_up_step(k):
        q = row_peer(k)
        gate, up = gate_up(q)
        q1_copy(q).start()
        rssend[q, :, 0:H] = gate.astype(jnp.bfloat16)
        rssend[q, :, H:2 * H] = up.astype(jnp.bfloat16)
        rs_copy(q).start()

    loop(R, gate_up_step, 1)
    gate, up = gate_up(r)
    guown[:, 0:H] = gate
    guown[:, H:2 * H] = up

    def transpose_step(q):
        ytbuf[:, pl.ds(pl.multiple_of(q * T, T), T)] = ybuf[q].T

    loop(Z, transpose_step)

    squares = st1send[r]
    for k in range(1, R):
        q = row_peer(k)
        q1_arrival(q).wait_recv()
        squares = squares + st1recv[q]
    inv_norm = to_column(lax.rsqrt(squares / features + norm_eps)[0:1, :])
    invbuf[...] = inv_norm

    def gate_sum_step(k):
        q = row_peer(k)
        rs_arrival(q).wait_recv()
        guown[...] += rsrecv[q].astype(jnp.float32)

    loop(R, gate_sum_step, 1)
    gate = guown[:, 0:H] * invbuf[...]
    up = guown[:, H:2 * H] * invbuf[...]
    gatebuf[...] = gate
    upbuf[...] = up
    hbuf[r] = (gate * jax.nn.sigmoid(gate) * up).astype(jnp.bfloat16)

    def h_copy(q):
        return copy(hbuf.at[r], hbuf.at[r], h_s.at[q], h_r.at[r], row_device(q))

    def h_arrival(q):
        return copy(hbuf.at[q], hbuf.at[q], h_s.at[q], h_r.at[q], row_device(q))

    for k in range(1, R):
        h_copy(row_peer(k)).start()

    def ob_copy(q):
        return copy(osend.at[q, other], osib.at[q], ob_s.at[q], ob_r.at[q], sibling)

    def ob_arrival(q):
        return copy(osend.at[q, mine], osib.at[q], ob_s.at[q], ob_r.at[q], sibling)

    def oz_copy(q):
        return copy(zsend.at[q], zrecv.at[d], oz_s.at[q], oz_r.at[d], depth_device(q))

    def oz_arrival(q):
        return copy(zsend.at[q], zrecv.at[q], oz_s.at[q], oz_r.at[q], depth_device(q))

    def down_step(k):
        q = depth_peer(k)

        @pl.when(q != r)
        def _():
            h_arrival(q).wait_recv()

        osend[q] = dot(hbuf[q], wd_ref[...]).astype(jnp.bfloat16)
        ob_copy(q).start()

    loop(Z + 1, down_step, 1)

    def pair_step(k):
        q = depth_peer(k)
        ob_arrival(q).wait_recv()
        zsend[q] = (
            osend[q, mine].astype(jnp.float32) + osib[q].astype(jnp.float32)
        ).astype(jnp.bfloat16)
        oz_copy(q).start()

    loop(Z, pair_step, 1)
    ob_arrival(d).wait_recv()
    oown[...] = osend[d, mine].astype(jnp.float32) + osib[d].astype(jnp.float32)

    def transpose_hidden_step(q):
        htbuf[:, pl.ds(pl.multiple_of(q * T, T), T)] = hbuf[q].T

    loop(R, transpose_hidden_step)

    def depth_sum_step(k):
        q = depth_peer(k)
        oz_arrival(q).wait_recv()
        oown[...] += zrecv[q].astype(jnp.float32)

    loop(Z, depth_sum_step, 1)
    ysend[...] = oown[...].astype(jnp.bfloat16)

    def block(j):
        return pl.ds(pl.multiple_of(j * B, 16), B)

    def oy_copy(j):
        return copy(ysend.at[block(j)], yrecv.at[yh], oy_s.at[j], oy_r.at[yh], y_device(j))

    def oy_arrival(j):
        return copy(ysend.at[block(j)], yrecv.at[j], oy_s.at[j], oy_r.at[j], y_device(j))

    for k in range(1, YH):
        oy_copy(y_peer(k)).start()
    output = oown[block(yh)] + xbuf[d, slot(core, yh)].astype(jnp.float32)
    for k in range(1, YH):
        j = y_peer(k)
        oy_arrival(j).wait_recv()
        output = output + yrecv[j].astype(jnp.float32)
    obuf[d, slot(core, yh)] = output.astype(jnp.bfloat16)

    def ay_copy(j):
        part = obuf.at[d, slot(core, yh)]
        return copy(part, part, ay_s.at[j], ay_r.at[yh], y_device(j))

    def ay_arrival(j):
        part = obuf.at[d, slot(core, j)]
        return copy(part, part, ay_s.at[j], ay_r.at[j], y_device(j))

    for k in range(1, YH):
        ay_copy(y_peer(k)).start()
    for k in range(1, YH):
        ay_arrival(y_peer(k)).wait_recv()
    a_copy, a_arrival, as_copy, as_arrival = gather_over_depth(obuf, az_s, az_r, ab_s, ab_r)
    for k in near:
        a_copy(k).start()
    as_copy(0).start()
    for k in near:
        a_arrival(k).wait_recv()
        as_copy(k).start()

    head = gvbuf[1:2, :]

    def stat_step(k):
        q = depth_peer(Z - k)
        as_arrival(k).wait_recv()
        wide = obuf[q].astype(jnp.float32)
        st2send[pl.ds(q, 1), :] = to_lanes(jnp.sum(wide * wide, axis=1, keepdims=True))
        st2send[pl.ds(Z + q, 1), :] = to_lanes(jnp.sum(wide * head, axis=1, keepdims=True))

    loop(Z, stat_step)

    def q2_copy(q):
        return copy(st2send, st2recv.at[r], q2_s.at[q], q2_r.at[r], row_device(q))

    def q2_arrival(q):
        return copy(st2send, st2recv.at[q], q2_s.at[q], q2_r.at[q], row_device(q))

    for k in range(1, R):
        q2_copy(row_peer(k)).start()

    target = tg2send[...]
    for k in range(1, Z):
        t2_arrival(k).wait_recv()
        target = target + tg2[depth_peer(Z - k)]

    sums = st2send[...]
    for k in range(1, R):
        q = row_peer(k)
        q2_arrival(q).wait_recv()
        sums = sums + st2recv[q]
    inv_final = lax.rsqrt(sums[0:Z] / features + norm_eps)
    values = sums[Z:2 * Z] * inv_final
    val_ref[...] = values
    slope = jnp.clip(values - target[0:Z], -huber_delta, huber_delta)
    abuf[...] = inv_final * slope
    bbuf[...] = inv_final * inv_final * (slope * values / features)

    def gh_copy(q):
        return copy(ghsend.at[q], ghrecv.at[r], gh_s.at[q], gh_r.at[r], row_device(q))

    def gh_arrival(q):
        return copy(ghsend.at[q], ghrecv.at[q], gh_s.at[q], gh_r.at[q], row_device(q))

    gvsend[...] = jnp.zeros_like(gvsend)

    def grad_hidden(q):
        wide = obuf[q].astype(jnp.float32)
        scale = to_column(abuf[pl.ds(q, 1), :])
        shrink = to_column(bbuf[pl.ds(q, 1), :])
        grad = (scale * head - shrink * wide).astype(jnp.bfloat16)
        gobuf[q] = grad
        gvsend[...] += jnp.broadcast_to(
            jnp.sum(wide * scale, axis=0, keepdims=True), gvsend.shape
        )
        return lax.dot_general(
            grad, wd_ref[...], (((1,), (1,)), ((), ())), preferred_element_type=jnp.float32
        )

    def grad_hidden_step(k):
        q = row_peer(k)
        ghsend[q] = grad_hidden(q).astype(jnp.bfloat16)
        gh_copy(q).start()

    loop(R, grad_hidden_step, 1)
    ghown[...] = grad_hidden(r)

    go_copy = copy(gvsend, gvrecv, go_s, go_r, partner)

    @pl.when(diagonal)
    def _():
        gvrecv[...] = gvsend[...]

    @pl.when(jnp.logical_not(diagonal))
    def _():
        go_copy.start()

    def hidden_sum_step(k):
        q = row_peer(k)
        gh_arrival(q).wait_recv()
        ghown[...] += ghrecv[q].astype(jnp.float32)

    loop(R, hidden_sum_step, 1)
    gate = gatebuf[...]
    up = upbuf[...]
    sig = jax.nn.sigmoid(gate)
    grad = ghown[...] * invbuf[...]
    ggbuf[r, :, 0:H] = (grad * up * sig * (1.0 + gate * (1.0 - sig))).astype(jnp.bfloat16)
    ggbuf[r, :, H:2 * H] = (grad * gate * sig).astype(jnp.bfloat16)

    def gg_copy(q):
        return copy(ggbuf.at[r], ggbuf.at[r], gg_s.at[q], gg_r.at[r], row_device(q))

    def gg_arrival(q):
        return copy(ggbuf.at[q], ggbuf.at[q], gg_s.at[q], gg_r.at[q], row_device(q))

    for k in range(1, R):
        gg_copy(row_peer(k)).start()

    tokens = Z * T
    tile = min(128, H)

    def down_weight_step(m):
        rows = pl.ds(pl.multiple_of(m * tile, tile), tile)
        dd_ref[rows, :] = dot(
            htbuf[rows, :], gobuf[...].reshape(tokens, F)
        ).astype(jnp.bfloat16)

    loop(H // tile, down_weight_step)

    for k in range(1, R):
        gg_arrival(row_peer(k)).wait_recv()

    tile_f = min(128, F)

    def weight_step(m):
        rows = pl.ds(pl.multiple_of(m * tile_f, tile_f), tile_f)
        both = dot(ytbuf[rows, :], ggbuf[...].reshape(tokens, 2 * H)).astype(jnp.bfloat16)
        dg_ref[rows, :] = both[:, 0:H]
        du_ref[rows, :] = both[:, H:2 * H]

    loop(F // tile_f, weight_step)

    @pl.when(jnp.logical_not(diagonal))
    def _():
        go_copy.wait_recv()
    gval_ref[...] = gvrecv[...]

    for j in range(YH):
        @pl.when(jnp.logical_not(diagonal & (yh == j)))
        def _():
            first_copy(j).wait_send()

    @pl.when(jnp.logical_not(diagonal))
    def _():
        gv_copy.wait_send()
        go_copy.wait_send()

    def row_sends(k):
        q = row_peer(k)
        t1_copy(k).wait_send()
        rs_copy(q).wait_send()
        q1_copy(q).wait_send()
        h_copy(q).wait_send()
        q2_copy(q).wait_send()
        gh_copy(q).wait_send()
        gg_copy(q).wait_send()

    loop(R, row_sends, 1)

    def depth_sends(k):
        t2_copy(k).wait_send()
        z_copy(k).wait_send()
        a_copy(k).wait_send()
        oz_copy(depth_peer(k)).wait_send()

    loop(Z, depth_sends, 1)

    def pair_sends(k):
        s_copy(k).wait_send()
        as_copy(k).wait_send()
        ob_copy(k).wait_send()

    loop(Z, pair_sends)

    def y_sends(k):
        oy_copy(y_peer(k)).wait_send()
        ay_copy(y_peer(k)).wait_send()

    loop(YH, y_sends, 1)


def build(mesh):
    R, C, Z = mesh.shape["row"], mesh.shape["col"], mesh.shape["depth"]
    YH = C // 2

    def per_device(residual, pre_gain, w_gate, w_up, w_down, value_head, sample_index, return_table):
        B, F = residual.shape
        H = w_gate.shape[1]
        T = C * B
        r = lax.axis_index("row")
        d = lax.axis_index("depth")
        lane = (r % 2) * (YH * B) + (r // 2) * B
        target = jnp.take(return_table, sample_index)
        rows = max(8, Z)
        tile = lax.dynamic_update_slice(
            jnp.zeros((rows, T), jnp.float32), target[None, :], (d, lane)
        )
        gv = jnp.zeros((8, F), jnp.float32).at[0].set(pre_gain).at[1].set(value_head)

        bf, f32 = jnp.bfloat16, jnp.float32
        V = pltpu.VMEM
        dma = lambda *shape: pltpu.SemaphoreType.DMA(shape)
        half = YH * B
        scratch = [
            V((Z, T, F), bf), V((Z, T, F), bf), V((F, Z * T), bf),
            V((R, T, 2 * H), bf), V((R, T, 2 * H), bf), V((T, 2 * H), f32),
            V((R, 8, T), f32), V((R, 8, T), f32),
            V((R, T, H), bf), V((H, R * T), bf),
            V((T, H), f32), V((T, H), f32), V((T, 1), f32),
            V((Z, T, F), bf), V((Z, half, F), bf), V((half, F), f32),
            V((Z, half, F), bf), V((Z, half, F), bf), V((half, F), bf), V((YH, B, F), bf),
            V((Z, T, F), bf),
            V((2 * Z, T), f32), V((R, 2 * Z, T), f32), V((Z, T), f32), V((Z, T), f32),
            V((Z, T, F), bf), V((R, T, H), bf), V((R, T, H), bf), V((T, H), f32),
            V((R, T, 2 * H), bf),
            V((8, F), f32), V((8, F), f32), V((8, F), f32),
            V((R, rows, T), f32), V((rows, T), f32), V((Z, rows, T), f32),
            dma(YH), dma(YH), dma(), dma(), dma(R), dma(R), dma(Z), dma(Z),
            dma(Z), dma(Z), dma(Z), dma(Z), dma(R), dma(R), dma(R), dma(R), dma(R), dma(R),
            dma(Z), dma(Z), dma(Z), dma(Z), dma(YH), dma(YH), dma(YH), dma(YH),
            dma(Z), dma(Z), dma(Z), dma(Z),
            dma(R), dma(R), dma(R), dma(R), dma(R), dma(R), dma(), dma(),
        ]
        vmem = pl.BlockSpec(memory_space=pltpu.VMEM)
        dg, du, dd, values, gval = pl.pallas_call(
            functools.partial(kernel, R, YH, Z, B, F, H),
            out_shape=(
                jax.ShapeDtypeStruct((F, H), bf),
                jax.ShapeDtypeStruct((F, H), bf),
                jax.ShapeDtypeStruct((H, F), bf),
                jax.ShapeDtypeStruct((Z, T), f32),
                jax.ShapeDtypeStruct((8, F), f32),
            ),
            in_specs=[vmem] * 6,
            out_specs=(vmem,) * 5,
            scratch_shapes=scratch,
            compiler_params=pltpu.CompilerParams(
                collective_id=0, has_side_effects=True, vmem_limit_bytes=40 * 1024 * 1024
            ),
        )(residual, gv, tile, w_gate, w_up, w_down)
        values = lax.dynamic_slice(values, (d, lane), (1, B))[0]
        return values, dg, du, dd, gval[0]

    return per_device


def solution(mesh):
    placed = (
        P(("row", "depth"), "col"),
        P("col"),
        P("row", ("col", "depth")),
        P("row", ("col", "depth")),
        P(("col", "depth"), "row"),
        P("col"),
        P(("row", "depth")),
        P(),
    )
    return jax.shard_map(
        build(mesh),
        mesh=mesh,
        in_specs=placed,
        out_specs=(
            P(("row", "depth")),
            P("row", ("col", "depth")),
            P("row", ("col", "depth")),
            P(("col", "depth"), "row"),
            P("col"),
        ),
        check_vma=False,
    )
```

time: 824 us -> 140 us (0.17)
  the two profiles are of different devices: /device:TPU:16 before, /device:TPU:1 now
where the time goes in v1:
time: 140 us; the launch traced here: 139 us
  Pallas kernels  132 us (94%)
  local copies, waits for them, and re-layouts  6.64 us (5%)
    pallas_call x1, Pallas kernels, per_device(): pl.pallas_call(functools.partial(kernel, R, YH, Z, B, F, H), out_shape=(j...  132 us
    unnamed x19, local copies, waits for them, and re-layouts  4.59 us

profile of v1, /device:TPU:1, one launch (start us, length us, event | category | flops | bytes accessed | tf_op | source)
XLA Modules:
  0.0 139.2 jit_solution(7843155681641308796)
XLA Ops:
  0.6 0.0 copy-start
  0.7 0.0 copy-start.7
  0.7 0.7 copy-done.7
  1.4 0.2 copy-done
  1.5 0.0 copy-start.5
  1.5 0.0 copy-start.1
  1.5 0.0 copy-start.2
  1.5 0.7 gather_fusion
  2.2 0.0 copy-start.4
  2.2 0.2 dynamic_update_slice.3.tgt_ref
  2.4 0.0 copy-done.5
  2.4 0.0 copy-start.6
  2.5 0.7 copy-done.6
  3.2 0.0 copy-done.1
  3.2 0.0 copy-done.2
  3.2 0.0 copy-done.4
  3.2 0.0 copy-start.3
  3.2 0.9 copy-done.3
  4.1 131.8 %shard_map.119 = (bf16[512,256]{1,0:T(8,128)(2,1)S(1)}, bf16[512,256]{1,0:T(8,128)(2,1)S(1)}, bf16[256,512]{1,0:T(8,128)(2,1)S(1)}, f32[8,128]{1,0:T(8,128)S(1)}, f32[8,512]{1,0:T(8,128)S(1)}) custom-call(bf16[16,512]{1,0:T(8,128)(2,1)S(1)} %copy-done.4, f32[8,512]{1,0:T(8,128)S(1)} %scatter.9.gv_ref, f32[8,128]{1,0:T(8,128)S(1)} %dynamic_update_slice.3.tgt_ref, ...), custom_call_target="tpu_custom_call" | custom-call | tf_op jit(solution)/shard_map/pallas_call | solution.py:597
  136.0 0.6 dynamic-slice_bitcast_fusion
  136.6 0.6 slice.32
  137.1 0.7 copy.18
  137.8 0.7 copy.19
  138.5 0.7 copy.20
  (6 shorter events, 0.1 us)
Async XLA Ops:
  0.6 0.9 copy-start
  0.7 0.7 copy-start.7
  1.5 0.9 copy-start.5
  1.5 1.6 %copy-start.1 = (bf16[512,256]{1,0:T(8,128)(2,1)S(1)}, bf16[512,256]{1,0:T(8,128)(2,1)}, u32[]{:S(2)}) copy-start(bf16[512,256]{1,0:T(8,128)(2,1)} %wg_ref.1) | copy-start | bytes 786436
  1.5 1.6 %copy-start.2 = (bf16[512,256]{1,0:T(8,128)(2,1)S(1)}, bf16[512,256]{1,0:T(8,128)(2,1)}, u32[]{:S(2)}) copy-start(bf16[512,256]{1,0:T(8,128)(2,1)} %wu_ref.1) | copy-start | bytes 786436
  2.2 1.0 copy-start.4
  2.4 0.7 copy-start.6
  3.2 1.0 copy-start.3

commit v2 on v0

v2 whole, which is shorter than its diff:
```python
import functools

import jax
import jax.numpy as jnp
from jax import lax
from jax.experimental import pallas as pl
from jax.experimental.pallas import tpu as pltpu
from jax.sharding import PartitionSpec as P

MESH = pl.DeviceIdType.MESH
norm_eps = 1e-06
huber_delta = 1.0


def rem(value, size):
    return lax.rem(value, jnp.int32(size))


def dot(left, right):
    return jnp.dot(left, right, preferred_element_type=jnp.float32)


def dot_t(left, right):
    return lax.dot_general(
        left, right, (((1,), (1,)), ((), ())), preferred_element_type=jnp.float32
    )


def kernel(
    R, YH, Z, B, F, H,
    x_ref, gv_ref, tgt_ref, wg_ref, wu_ref, wd_ref,
    dg_ref, du_ref, dd_ref, val_ref, gval_ref,
    xbuf, ybuf, y2buf, y2t, wgbuf, wubuf, wdbuf, gvbuf, tg1, tgsend, tg2,
    acc, rssend, rsrecv, st1send, st1recv, hbuf, ht, gubuf, coef,
    osend, osib, oown, zsend, zrecv, ysend, yrecv, outblk, obuf,
    st2send, st2recv, gobuf, go2buf, ghpart, ghsend, ghrecv, ghbuf, ggbuf, gsum, grecv,
    x1s, x1r, x2s, x2r, x3s, x3r, gvs, gvr, gbs, gbr, t1s, t1r, t2s, t2r,
    wls, wgs, wgr, wus, wur, wds, wdr, q1s, q1r, rss, rsr, y2s, y2r, hs, hr, gus, gur,
    obs, obr, ozs, ozr, oys, oyr, a1s, a1r, a2s, a2r, a3s, a3r, q2s, q2r,
    gos, gor, g1s, g1r, ghs, ghr, gvos, gvor,
):
    XN, YQ = R // 2, YH // 2
    N = Z * 2 * B
    L = N // 2
    features = R * F
    r = lax.axis_index("row")
    c = lax.axis_index("col")
    d = lax.axis_index("depth")
    x = rem(r, XN)
    yl = lax.div(r, jnp.int32(XN))
    core = rem(c, 2)
    yh = lax.div(c, jnp.int32(2))
    side = lax.div(yh, jnp.int32(YQ))
    mloc = rem(yh, YQ)
    home = yl == side
    sibling = (r, 2 * yh + 1 - core, d)
    ypair = ((1 - yl) * XN + x, c, d)

    def copy(src, dst, send, recv, device):
        return pltpu.make_async_remote_copy(
            src_ref=src, dst_ref=dst, send_sem=send, recv_sem=recv,
            device_id=device, device_id_type=MESH,
        )

    def row_peer(k):
        return rem(r + k, R)

    def depth_peer(k):
        return rem(d + k, Z)

    def x_peer(k):
        return rem(x + k, XN)

    def row_device(q):
        return (q, c, d)

    def depth_device(q):
        return (r, c, q)

    def x_device(q):
        return (yl * XN + q, c, d)

    def seat(q):
        return rem(q, XN) * 2 + lax.div(q, jnp.int32(XN))

    my_seat = x * 2 + yl

    def reader(j):
        return (side * XN + x, 2 * j + core, d)

    def owner(s, m):
        return (s * XN + x, 2 * (yl * YQ + m) + core, d)

    def is_owner(s, m):
        return (yl == s) & (yh == yl * YQ + m)

    def span(index, size):
        return pl.ds(pl.multiple_of(index * size, size), size)

    def block(depth, s):
        return pl.ds(pl.multiple_of(depth * (2 * B) + s * B, B), B)

    def loop(count, body, start=0):
        def step(k, carry):
            body(k)
            return carry
        lax.fori_loop(start, count, step, 0)

    eye = (
        lax.broadcasted_iota(jnp.int32, (L, L), 0)
        == lax.broadcasted_iota(jnp.int32, (L, L), 1)
    )

    def to_lanes(column):
        return jnp.sum(jnp.where(eye, column, 0.0), axis=0, keepdims=True)

    def to_column(lanes):
        return jnp.sum(jnp.where(eye, lanes, 0.0), axis=1, keepdims=True)

    barrier = pltpu.get_barrier_semaphore()

    def greet(device):
        pl.semaphore_signal(barrier, inc=1, device_id=device, device_id_type=MESH)

    for k in range(1, R):
        greet(row_device(row_peer(k)))
    for k in range(1, Z):
        greet(depth_device(depth_peer(k)))
    greet(sibling)
    for j in range(YH):
        @pl.when(jnp.logical_not(home & (yh == j)))
        def _():
            greet(reader(j))
    for s in range(2):
        for m in range(YQ):
            @pl.when(jnp.logical_not(is_owner(s, m)))
            def _():
                greet(owner(s, m))
    pl.semaphore_wait(
        barrier, (R - 1) + (Z - 1) + 1 + YH + 2 * YQ - jnp.where(home, 2, 0)
    )

    near = []
    for k in range(1, Z // 2 + 1):
        near.append(k)
        if Z - k > k:
            near.append(Z - k)

    class Gather:
        def __init__(self, src, buf, s1, r1, s2, r2, s3, r3):
            self.src, self.buf = src, buf
            self.sems = (s1, r1, s2, r2, s3, r3)

        def first(self, j):
            s1, r1 = self.sems[:2]
            return copy(
                self.src, self.buf.at[core, mloc, block(d, yl)],
                s1.at[j], r1.at[yl * YQ + mloc], reader(j),
            )

        def first_arrival(self, s, m):
            s1, r1 = self.sems[:2]
            return copy(
                self.src, self.buf.at[core, m, block(d, s)],
                s1.at[0], r1.at[s * YQ + m], owner(s, m),
            )

        def start(self):
            for j in range(YH):
                @pl.when(home & (yh == j))
                def _():
                    self.buf[core, mloc, block(d, yl)] = self.src[...]

                @pl.when(jnp.logical_not(home & (yh == j)))
                def _():
                    self.first(j).start()

        def piece(self, which, q):
            return self.buf.at[which, :, span(q, 2 * B)]

        def z_copy(self, k):
            part = self.piece(core, d)
            return copy(
                part, part, self.sems[2].at[k], self.sems[3].at[k],
                depth_device(depth_peer(k)),
            )

        def z_arrival(self, k):
            q = depth_peer(Z - k)
            part = self.piece(core, q)
            return copy(part, part, self.sems[2].at[k], self.sems[3].at[k], depth_device(q))

        def s_copy(self, k):
            part = self.piece(core, depth_peer(Z - k))
            return copy(part, part, self.sems[4].at[k], self.sems[5].at[k], sibling)

        def s_arrival(self, k):
            part = self.piece(1 - core, depth_peer(Z - k))
            return copy(part, part, self.sems[4].at[k], self.sems[5].at[k], sibling)

        def spread(self):
            for s in range(2):
                for m in range(YQ):
                    @pl.when(jnp.logical_not(is_owner(s, m)))
                    def _():
                        self.first_arrival(s, m).wait_recv()
            for k in near:
                self.z_copy(k).start()
            self.s_copy(0).start()

        def pass_on(self):
            for k in near:
                self.z_arrival(k).wait_recv()
                self.s_copy(k).start()

        def arrived(self):
            for k in [0] + near:
                self.s_arrival(k).wait_recv()

        def drain(self):
            for j in range(YH):
                @pl.when(jnp.logical_not(home & (yh == j)))
                def _():
                    self.first(j).wait_send()
            for k in range(1, Z):
                self.z_copy(k).wait_send()
            for k in range(Z):
                self.s_copy(k).wait_send()

    gx = Gather(x_ref, xbuf, x1s, x1r, x2s, x2r, x3s, x3r)
    gx.start()

    def gv_copy(j):
        return copy(gv_ref, gvbuf.at[core, mloc], gvs.at[j], gvr.at[mloc], reader(j))

    def gv_arrival(m):
        return copy(gv_ref, gvbuf.at[core, m], gvs.at[0], gvr.at[m], owner(0, m))

    for j in range(YH):
        @pl.when((yl == 0) & home & (yh == j))
        def _():
            gvbuf[core, mloc] = gv_ref[...]

        @pl.when((yl == 0) & jnp.logical_not(home & (yh == j)))
        def _():
            gv_copy(j).start()

    def local_weights():
        return (
            pltpu.make_async_copy(wg_ref, wgbuf.at[x], wls.at[0]),
            pltpu.make_async_copy(wu_ref, wubuf.at[x], wls.at[1]),
            pltpu.make_async_copy(wd_ref, wdbuf.at[x], wls.at[2]),
        )

    for one in local_weights():
        one.start()

    def w_copy(ref, buf, send, recv, k):
        return copy(ref, buf.at[x], send.at[k], recv.at[k], x_device(x_peer(k)))

    def w_arrival(ref, buf, send, recv, k):
        q = x_peer(XN - k)
        return copy(ref, buf.at[q], send.at[k], recv.at[k], x_device(q))

    gate_w = (wg_ref, wgbuf, wgs, wgr)
    up_w = (wu_ref, wubuf, wus, wur)
    down_w = (wd_ref, wdbuf, wds, wdr)
    for k in range(1, XN):
        w_copy(*gate_w, k).start()
        w_copy(*up_w, k).start()

    t1_copy = copy(tgt_ref, tg1, t1s, t1r, ypair)
    t1_copy.start()

    gx.spread()

    for m in range(YQ):
        @pl.when(jnp.logical_not((yl == 0) & is_owner(0, m)))
        def _():
            gv_arrival(m).wait_recv()
    gb_copy = copy(gvbuf.at[core], gvbuf.at[core], gbs, gbr, sibling)
    gb_arrival = copy(gvbuf.at[1 - core], gvbuf.at[1 - core], gbs, gbr, sibling)
    gb_copy.start()

    t1_copy.wait_recv()
    tgsend[...] = tgt_ref[...] + tg1[...]

    def t2_copy(k):
        return copy(tgsend, tg2.at[d], t2s.at[k], t2r.at[k], depth_device(depth_peer(k)))

    def t2_arrival(k):
        q = depth_peer(Z - k)
        return copy(tgsend, tg2.at[q], t2s.at[k], t2r.at[k], depth_device(q))

    for k in range(1, Z):
        t2_copy(k).start()

    gx.pass_on()

    for one in local_weights():
        one.wait()
    for k in range(1, XN):
        w_arrival(*gate_w, k).wait_recv()
        w_arrival(*up_w, k).wait_recv()
    for k in range(1, XN):
        w_copy(*down_w, k).start()

    def gate_up(which, m):
        fl = 2 * m + which
        wide = xbuf[which, m].astype(jnp.float32)
        scaled = (wide * gvbuf[which, m, 0:1, :]).astype(jnp.bfloat16)
        ybuf[fl] = scaled
        acc[:, 0:H] += dot(scaled, wgbuf[fl])
        acc[:, H:2 * H] += dot(scaled, wubuf[fl])
        squares = jnp.sum(wide * wide, axis=1, keepdims=True)
        for s in range(2):
            st1send[s:s + 1, :] += to_lanes(squares[s * L:(s + 1) * L])

    acc[...] = jnp.zeros_like(acc)
    st1send[...] = jnp.zeros_like(st1send)
    loop(YQ, lambda m: gate_up(core, m))
    gb_arrival.wait_recv()
    gx.arrived()
    loop(YQ, lambda m: gate_up(1 - core, m))

    rs_copy = copy(rssend, rsrecv, rss, rsr, ypair)
    rssend[...] = acc[span(1 - yl, L)].astype(jnp.bfloat16)

    def q1_copy(q):
        return copy(st1send, st1recv.at[r], q1s.at[q], q1r.at[r], row_device(q))

    def q1_arrival(q):
        return copy(st1send, st1recv.at[q], q1s.at[q], q1r.at[q], row_device(q))

    pair_row = (1 - yl) * XN + x
    q1_copy(pair_row).start()
    rs_copy.start()
    for k in range(1, R):
        q = row_peer(k)

        @pl.when(q != pair_row)
        def _():
            q1_copy(q).start()
    st1recv[r] = st1send[...]

    def y2_copy(k):
        q = x_peer(k)
        return copy(ybuf.at[q], y2buf.at[x], y2s.at[k], y2r.at[k], x_device(q))

    def y2_arrival(k):
        q = x_peer(XN - k)
        return copy(ybuf.at[x], y2buf.at[q], y2s.at[k], y2r.at[k], x_device(q))

    for k in range(1, XN):
        y2_copy(k).start()

    q1_arrival(pair_row).wait_recv()
    squares = st1send[...] + st1recv[pair_row]
    inv_lanes = lax.rsqrt(squares / features + norm_eps)
    inv_mine = jnp.where(yl == 0, inv_lanes[0:1, :], inv_lanes[1:2, :])
    inv_norm = to_column(inv_mine)
    rs_copy.wait_recv()
    total = (acc[span(yl, L)] + rsrecv[...].astype(jnp.float32)) * inv_norm
    gate, up = total[:, 0:H], total[:, H:2 * H]
    hbuf[my_seat] = (gate * jax.nn.sigmoid(gate) * up).astype(jnp.bfloat16)

    def h_copy(q):
        part = hbuf.at[my_seat]
        return copy(part, part, hs.at[q], hr.at[r], row_device(q))

    def h_arrival(q):
        part = hbuf.at[seat(q)]
        return copy(part, part, hs.at[q], hr.at[q], row_device(q))

    def gu_copy(q):
        part = gubuf.at[my_seat]
        return copy(part, part, gus.at[q], gur.at[r], row_device(q))

    def gu_arrival(q):
        part = gubuf.at[seat(q)]
        return copy(part, part, gus.at[q], gur.at[q], row_device(q))

    h_copy(pair_row).start()
    gubuf[my_seat] = total.astype(jnp.bfloat16)

    for k in range(1, XN):
        w_arrival(*down_w, k).wait_recv()

    def ob_copy(s):
        part = pl.ds(pl.multiple_of(s * L, L), L)
        return copy(osend.at[:, part], osib.at[:, part], obs.at[s], obr.at[s], sibling)

    def down(s):
        rows = span(s, L)
        act = hbuf[x * 2 + s]
        for m in range(YQ):
            osend[m, rows] = dot(act, wdbuf[2 * m + 1 - core]).astype(jnp.bfloat16)
        ob_copy(s).start()
        for m in range(YQ):
            oown[m, rows] = dot(act, wdbuf[2 * m + core])

    down(yl)
    for k in range(1, R):
        q = row_peer(k)

        @pl.when(q != pair_row)
        def _():
            h_copy(q).start()
        gu_copy(q).start()

    def oz_copy(q):
        return copy(
            zsend.at[:, span(q, 2 * B)], zrecv.at[d], ozs.at[q], ozr.at[d], depth_device(q)
        )

    def oz_arrival(q):
        return copy(
            zsend.at[:, span(q, 2 * B)], zrecv.at[q], ozs.at[q], ozr.at[q], depth_device(q)
        )

    def pair_sum(s):
        rows = span(s, L)
        ob_copy(s).wait_recv()
        for m in range(YQ):
            both = oown[m, rows] + osib[m, rows].astype(jnp.float32)
            oown[m, rows] = both
            zsend[m, rows] = both.astype(jnp.bfloat16)
        for i in range(Z // 2):
            q = s * (Z // 2) + rem(d + i, Z // 2)

            @pl.when(q != d)
            def _():
                oz_copy(q).start()

    pair_sum(yl)
    h_arrival(pair_row).wait_recv()
    down(1 - yl)
    pair_sum(1 - yl)

    y2buf[x] = ybuf[x]
    y2t[:, span(x, N)] = ybuf[x].T
    for k in range(1, XN):
        q = x_peer(XN - k)
        y2_arrival(k).wait_recv()
        y2t[:, span(q, N)] = y2buf[q].T

    mine = span(d, 2 * B)
    for k in near:
        q = depth_peer(k)
        oz_arrival(q).wait_recv()
        for m in range(YQ):
            oown[m, mine] += zrecv[q, m].astype(jnp.float32)
    for m in range(YQ):
        ysend[m] = oown[m, mine].astype(jnp.bfloat16)

    def oy_copy(s, m):
        return copy(
            ysend.at[m, pl.ds(s * B, B)], yrecv.at[yh], oys.at[s * YQ + m], oyr.at[yh],
            owner(s, m),
        )

    def oy_arrival(j):
        return copy(ysend.at[0, pl.ds(0, B)], yrecv.at[j], oys.at[0], oyr.at[j], reader(j))

    for s in range(2):
        for m in range(YQ):
            @pl.when(is_owner(s, m))
            def _():
                yrecv[yh] = ysend[m, s * B:(s + 1) * B]

            @pl.when(jnp.logical_not(is_owner(s, m)))
            def _():
                oy_copy(s, m).start()
    output = x_ref[...].astype(jnp.float32)
    for j in range(YH):
        @pl.when(jnp.logical_not(home & (yh == j)))
        def _():
            oy_arrival(j).wait_recv()
        output = output + yrecv[j].astype(jnp.float32)
    outblk[...] = output.astype(jnp.bfloat16)

    ga = Gather(outblk, obuf, a1s, a1r, a2s, a2r, a3s, a3r)
    ga.start()

    ht[:, span(my_seat, L)] = hbuf[my_seat].T

    def hidden_step(k):
        q = row_peer(k)

        @pl.when(q != pair_row)
        def _():
            h_arrival(q).wait_recv()
        ht[:, span(seat(q), L)] = hbuf[seat(q)].T

    loop(R, hidden_step, 1)

    ga.spread()

    def coef_of(q):
        s = seat(q)
        first = rem(q, XN)
        parity = lax.div(q, jnp.int32(XN))
        sums = st1recv[first] + st1recv[first + XN]
        lanes = jnp.where(parity == 0, sums[0:1, :], sums[1:2, :])
        inv = to_column(lax.rsqrt(lanes / features + norm_eps))
        both = gubuf[s].astype(jnp.float32)
        gate, up = both[:, 0:H], both[:, H:2 * H]
        sig = jax.nn.sigmoid(gate)
        coef[s, :, 0:H] = inv * (up * sig * (1.0 + gate * (1.0 - sig)))
        coef[s, :, H:2 * H] = inv * (gate * sig)

    for k in range(1, R):
        q = row_peer(k)

        @pl.when(q != pair_row)
        def _():
            q1_arrival(q).wait_recv()

    def coef_step(k):
        q = row_peer(k)
        gu_arrival(q).wait_recv()
        coef_of(q)

    loop(R, coef_step, 1)
    coef_of(r)

    ga.pass_on()

    target = tgsend[...]
    for k in range(1, Z):
        t2_arrival(k).wait_recv()
        target = target + tg2[depth_peer(Z - k)]

    def stats(which, m):
        wide = obuf[which, m].astype(jnp.float32)
        head = gvbuf[which, m, 1:2, :]
        squares = jnp.sum(wide * wide, axis=1, keepdims=True)
        products = jnp.sum(wide * head, axis=1, keepdims=True)
        for s in range(2):
            part = slice(s * L, (s + 1) * L)
            st2send[s:s + 1, :] += to_lanes(squares[part])
            st2send[2 + s:3 + s, :] += to_lanes(products[part])

    st2send[...] = jnp.zeros_like(st2send)
    loop(YQ, lambda m: stats(core, m))
    ga.arrived()
    loop(YQ, lambda m: stats(1 - core, m))
    q2_copy = copy(st2send, st2recv, q2s, q2r, ypair)
    q2_copy.start()
    q2_copy.wait_recv()
    sums = st2send[...] + st2recv[...]
    inv_final = lax.rsqrt(sums[0:2] / features + norm_eps)
    values = sums[2:4] * inv_final
    val_ref[...] = jnp.broadcast_to(values[None], (4, 2, L)).reshape(8, L)
    slope = jnp.clip(values - target[0:2], -huber_delta, huber_delta)
    scale_lanes = inv_final * slope
    shrink_lanes = inv_final * inv_final * (slope * values / features)
    scale = jnp.concatenate([to_column(scale_lanes[s:s + 1]) for s in range(2)], axis=0)
    shrink = jnp.concatenate([to_column(shrink_lanes[s:s + 1]) for s in range(2)], axis=0)

    def go_copy(k):
        q = x_peer(k)
        return copy(gobuf.at[q], go2buf.at[x], gos.at[k], gor.at[k], x_device(q))

    def go_arrival(k):
        q = x_peer(XN - k)
        return copy(gobuf.at[x], go2buf.at[q], gos.at[k], gor.at[k], x_device(q))

    gsum[...] = jnp.zeros_like(gsum)
    ghpart[...] = jnp.zeros_like(ghpart)

    def grad_output(fl):
        which = rem(fl, 2)
        m = lax.div(fl, jnp.int32(2))
        wide = obuf[which, m].astype(jnp.float32)
        head = gvbuf[which, m, 1:2, :]
        gobuf[fl] = (scale * head - shrink * wide).astype(jnp.bfloat16)
        gsum[pl.ds(fl, 1), :] = jnp.sum(wide * scale, axis=0, keepdims=True)
        ghpart[...] += dot_t(gobuf[fl], wdbuf[fl])

    loop(XN, grad_output)

    g1_copy = copy(ghsend, ghrecv, g1s, g1r, ypair)
    ghsend[...] = ghpart[span(1 - yl, L)].astype(jnp.bfloat16)
    g1_copy.start()
    for k in range(1, XN):
        go_copy(k).start()

    def gvo_copy(q):
        return copy(gsum, grecv.at[r], gvos.at[q], gvor.at[r], row_device(q))

    def gvo_arrival(q):
        return copy(gsum, grecv.at[q], gvos.at[q], gvor.at[q], row_device(q))

    def gh_copy(q):
        part = ghbuf.at[my_seat]
        return copy(part, part, ghs.at[q], ghr.at[r], row_device(q))

    def gh_arrival(q):
        part = ghbuf.at[seat(q)]
        return copy(part, part, ghs.at[q], ghr.at[q], row_device(q))

    go2buf[x] = gobuf[x]
    g1_copy.wait_recv()
    ghbuf[my_seat] = (
        ghpart[span(yl, L)] + ghrecv[...].astype(jnp.float32)
    ).astype(jnp.bfloat16)
    for k in range(1, R):
        gh_copy(row_peer(k)).start()
    for k in range(1, R):
        gvo_copy(row_peer(k)).start()
    grecv[r] = gsum[...]

    for k in range(1, XN):
        go_arrival(k).wait_recv()
    tokens = XN * N
    tile = min(128, H)

    def down_weight_step(i):
        rows = span(i, tile)
        dd_ref[rows, :] = dot(ht[rows, :], go2buf[...].reshape(tokens, F)).astype(jnp.bfloat16)

    loop(H // tile, down_weight_step)

    def gg_of(s):
        grad = ghbuf[s].astype(jnp.float32)
        ggbuf[s, :, 0:H] = (grad * coef[s, :, 0:H]).astype(jnp.bfloat16)
        ggbuf[s, :, H:2 * H] = (grad * coef[s, :, H:2 * H]).astype(jnp.bfloat16)

    gg_of(my_seat)

    def gg_step(k):
        q = row_peer(k)
        gh_arrival(q).wait_recv()
        gg_of(seat(q))

    loop(R, gg_step, 1)

    tile_f = min(128, F)

    def weight_step(i):
        rows = span(i, tile_f)
        both = dot(y2t[rows, :], ggbuf[...].reshape(tokens, 2 * H)).astype(jnp.bfloat16)
        dg_ref[rows, :] = both[:, 0:H]
        du_ref[rows, :] = both[:, H:2 * H]

    loop(F // tile_f, weight_step)

    for k in range(1, R):
        gvo_arrival(row_peer(k)).wait_recv()
    head_sum = grecv[side * XN]
    for k in range(1, XN):
        head_sum = head_sum + grecv[side * XN + k]
    pick = lax.broadcasted_iota(jnp.int32, head_sum.shape, 0) == c - side * XN
    gval_ref[...] = jnp.broadcast_to(
        jnp.sum(jnp.where(pick, head_sum, 0.0), axis=0, keepdims=True), gval_ref.shape
    )

    gx.drain()
    ga.drain()
    for j in range(YH):
        @pl.when((yl == 0) & jnp.logical_not(home & (yh == j)))
        def _():
            gv_copy(j).wait_send()
    gb_copy.wait_send()
    t1_copy.wait_send()
    rs_copy.wait_send()
    q2_copy.wait_send()
    g1_copy.wait_send()

    def x_sends(k):
        w_copy(*gate_w, k).wait_send()
        w_copy(*up_w, k).wait_send()
        w_copy(*down_w, k).wait_send()
        y2_copy(k).wait_send()
        go_copy(k).wait_send()

    loop(XN, x_sends, 1)

    def row_sends(k):
        q = row_peer(k)
        q1_copy(q).wait_send()
        h_copy(q).wait_send()
        gu_copy(q).wait_send()
        gh_copy(q).wait_send()
        gvo_copy(q).wait_send()

    loop(R, row_sends, 1)

    def depth_sends(k):
        t2_copy(k).wait_send()
        oz_copy(depth_peer(k)).wait_send()

    loop(Z, depth_sends, 1)
    for s in range(2):
        ob_copy(s).wait_send()
        for m in range(YQ):
            @pl.when(jnp.logical_not(is_owner(s, m)))
            def _():
                oy_copy(s, m).wait_send()


def build(mesh):
    R, C, Z = mesh.shape["row"], mesh.shape["col"], mesh.shape["depth"]
    YH, XN = C // 2, R // 2
    YQ = YH // 2

    def per_device(residual, pre_gain, w_gate, w_up, w_down, value_head, sample_index, return_table):
        B, F = residual.shape
        H = w_gate.shape[1]
        N = Z * 2 * B
        L = N // 2
        r = lax.axis_index("row")
        d = lax.axis_index("depth")
        place = d * (2 * B) + (r // XN) * B
        target = jnp.take(return_table, sample_index)
        tile = lax.dynamic_update_slice(
            jnp.zeros((8, L), jnp.float32), target[None, :], (place // L, place % L)
        )
        gv = jnp.zeros((8, F), jnp.float32).at[0].set(pre_gain).at[1].set(value_head)

        bf, f32 = jnp.bfloat16, jnp.float32
        V = pltpu.VMEM
        dma = lambda *shape: pltpu.SemaphoreType.DMA(shape)
        scratch = [
            V((2, YQ, N, F), bf), V((XN, N, F), bf), V((XN, N, F), bf), V((F, XN * N), bf),
            V((XN, F, H), bf), V((XN, F, H), bf), V((XN, H, F), bf),
            V((2, YQ, 8, F), f32), V((8, L), f32), V((8, L), f32), V((Z, 8, L), f32),
            V((N, 2 * H), f32), V((L, 2 * H), bf), V((L, 2 * H), bf),
            V((8, L), f32), V((R, 8, L), f32),
            V((R, L, H), bf), V((H, R * L), bf), V((R, L, 2 * H), bf), V((R, L, 2 * H), f32),
            V((YQ, N, F), bf), V((YQ, N, F), bf), V((YQ, N, F), f32),
            V((YQ, N, F), bf), V((Z, YQ, 2 * B, F), bf), V((YQ, 2 * B, F), bf), V((YH, B, F), bf),
            V((B, F), bf), V((2, YQ, N, F), bf),
            V((8, L), f32), V((8, L), f32),
            V((XN, N, F), bf), V((XN, N, F), bf), V((N, H), f32), V((L, H), bf), V((L, H), bf),
            V((R, L, H), bf), V((R, L, 2 * H), bf), V((8, F), f32), V((R, 8, F), f32),
            dma(YH), dma(2 * YQ), dma(Z), dma(Z), dma(Z), dma(Z),
            dma(YH), dma(YQ), dma(), dma(), dma(), dma(), dma(Z), dma(Z),
            dma(3), dma(XN), dma(XN), dma(XN), dma(XN), dma(XN), dma(XN),
            dma(R), dma(R), dma(), dma(), dma(XN), dma(XN), dma(R), dma(R), dma(R), dma(R),
            dma(2), dma(2), dma(Z), dma(Z), dma(2 * YQ), dma(YH),
            dma(YH), dma(2 * YQ), dma(Z), dma(Z), dma(Z), dma(Z), dma(), dma(),
            dma(XN), dma(XN), dma(), dma(), dma(R), dma(R), dma(R), dma(R),
        ]
        vmem = pl.BlockSpec(memory_space=pltpu.VMEM)
        hbm = pl.BlockSpec(memory_space=pl.ANY)
        dg, du, dd, values, gval = pl.pallas_call(
            functools.partial(kernel, R, YH, Z, B, F, H),
            out_shape=(
                jax.ShapeDtypeStruct((F, H), bf),
                jax.ShapeDtypeStruct((F, H), bf),
                jax.ShapeDtypeStruct((H, F), bf),
                jax.ShapeDtypeStruct((8, L), f32),
                jax.ShapeDtypeStruct((8, F), f32),
            ),
            in_specs=[vmem, vmem, vmem, hbm, hbm, hbm],
            out_specs=(vmem,) * 5,
            scratch_shapes=scratch,
            compiler_params=pltpu.CompilerParams(
                collective_id=0, has_side_effects=True, vmem_limit_bytes=40 * 1024 * 1024
            ),
        )(residual, gv, tile, w_gate, w_up, w_down)
        values = lax.dynamic_slice(values, (place // L, place % L), (1, B))[0]
        return values, dg, du, dd, gval[0]

    return per_device


def solution(mesh):
    placed = (
        P(("row", "depth"), "col"),
        P("col"),
        P("row", ("col", "depth")),
        P("row", ("col", "depth")),
        P(("col", "depth"), "row"),
        P("col"),
        P(("row", "depth")),
        P(),
    )
    return jax.shard_map(
        build(mesh),
        mesh=mesh,
        in_specs=placed,
        out_specs=(
            P(("row", "depth")),
            P("row", ("col", "depth")),
            P("row", ("col", "depth")),
            P(("col", "depth"), "row"),
            P("col"),
        ),
        check_vma=False,
    )
```

time: 824 us -> 133 us (0.16)
  the two profiles are of different devices: /device:TPU:16 before, /device:TPU:1 now
where the time goes in v2:
time: 133 us
  Pallas kernels  125 us (94%)
  local copies, waits for them, and re-layouts  6.61 us (5%)
    pallas_call x1, Pallas kernels, per_device(): pl.pallas_call(functools.partial(kernel, R, YH, Z, B, F, H), out_shape=(j...  125 us
    unnamed x19, local copies, waits for them, and re-layouts  4.56 us

profile of v2, /device:TPU:1, one launch (start us, length us, event | category | flops | bytes accessed | tf_op | source)
XLA Modules:
  0.0 132.7 jit_solution(16562182613278434737)
XLA Ops:
  0.6 0.0 copy-start
  0.7 0.0 copy-start.7
  0.7 0.6 copy-done.7
  1.4 0.2 copy-done
  1.5 0.0 copy-start.5
  1.5 0.0 copy-start.1
  1.5 0.0 copy-start.2
  1.5 0.7 gather_fusion
  2.2 0.0 copy-start.4
  2.2 0.2 dynamic_update_slice.3.tgt_ref
  2.4 0.0 copy-done.5
  2.4 0.0 copy-start.6
  2.5 0.7 copy-done.6
  3.2 0.0 copy-done.1
  3.2 0.0 copy-done.2
  3.2 0.0 copy-done.4
  3.2 0.0 copy-start.3
  3.2 0.9 copy-done.3
  4.1 125.3 %shard_map.119 = (bf16[512,256]{1,0:T(8,128)(2,1)S(1)}, bf16[512,256]{1,0:T(8,128)(2,1)S(1)}, bf16[256,512]{1,0:T(8,128)(2,1)S(1)}, f32[8,128]{1,0:T(8,128)S(1)}, f32[8,512]{1,0:T(8,128)S(1)}) custom-call(bf16[16,512]{1,0:T(8,128)(2,1)S(1)} %copy-done.4, f32[8,512]{1,0:T(8,128)S(1)} %scatter.9.gv_ref, f32[8,128]{1,0:T(8,128)S(1)} %dynamic_update_slice.3.tgt_ref, ...), custom_call_target="tpu_custom_call" | custom-call | tf_op jit(solution)/shard_map/pallas_call | solution.py:748
  129.4 0.6 dynamic-slice_bitcast_fusion
  130.0 0.6 slice.32
  130.6 0.7 copy.18
  131.3 0.7 copy.19
  132.0 0.7 copy.20
  (6 shorter events, 0.1 us)
Async XLA Ops:
  0.6 0.9 copy-start
  0.7 0.7 copy-start.7
  1.5 0.9 copy-start.5
  1.5 1.6 %copy-start.1 = (bf16[512,256]{1,0:T(8,128)(2,1)S(1)}, bf16[512,256]{1,0:T(8,128)(2,1)}, u32[]{:S(2)}) copy-start(bf16[512,256]{1,0:T(8,128)(2,1)} %wg_ref.1) | copy-start | bytes 786436
  1.5 1.6 %copy-start.2 = (bf16[512,256]{1,0:T(8,128)(2,1)S(1)}, bf16[512,256]{1,0:T(8,128)(2,1)}, u32[]{:S(2)}) copy-start(bf16[512,256]{1,0:T(8,128)(2,1)} %wu_ref.1) | copy-start | bytes 786436
  2.2 1.0 copy-start.4
  2.4 0.7 copy-start.6
  3.2 1.0 copy-start.3

commit v3 on v2

--- a/solution.py
+++ b/solution.py
@@ -30,19 +30,24 @@
     R, YH, Z, B, F, H,
     x_ref, gv_ref, tgt_ref, wg_ref, wu_ref, wd_ref,
     dg_ref, du_ref, dd_ref, val_ref, gval_ref,
-    xbuf, ybuf, y2buf, y2t, wgbuf, wubuf, wdbuf, gvbuf, tg1, tgsend, tg2,
+    xbuf, xzb, ybuf, y2buf, y2t, wgbuf, wubuf, wdbuf, gvbuf, tg1, tgsend, tg2,
     acc, rssend, rsrecv, st1send, st1recv, hbuf, ht, gubuf, coef,
-    osend, osib, oown, zsend, zrecv, ysend, yrecv, outblk, obuf,
-    st2send, st2recv, gobuf, go2buf, ghpart, ghsend, ghrecv, ghbuf, ggbuf, gsum, grecv,
-    x1s, x1r, x2s, x2r, x3s, x3r, gvs, gvr, gbs, gbr, t1s, t1r, t2s, t2r,
-    wls, wgs, wgr, wus, wur, wds, wdr, q1s, q1r, rss, rsr, y2s, y2r, hs, hr, gus, gur,
-    obs, obr, ozs, ozr, oys, oyr, a1s, a1r, a2s, a2r, a3s, a3r, q2s, q2r,
-    gos, gor, g1s, g1r, ghs, ghr, gvos, gvor,
+    osend, osib, oown, zsend, zra, yra, yrb, zrb, ysa, zsb, outblk, obuf, ozb,
+    st2send, st2recv, scsend, screcv, o2buf, gobuf, go2buf,
+    ghpart, ghsend, ghrecv, ghbuf, ggbuf, gsum, grecv,
+    x1, x2, x3, x4, x5, x6, x7, x8, x9, x10, x11, x12, gvs, gvr, gbs, gbr, t1s, t1r, t2s, t2r,
+    wls, wgs, wgr, wus, wur, wds, wdr, q1s, q1r, rss, rsr, y2s, y2r, ybs, ybr, hs, hr, gus, gur,
+    obs, obr, zas, zar, yas, yar, ybbs, ybbr, zbs, zbr,
+    a1, a2, a3, a4, a5, a6, a7, a8, a9, a10, a11, a12, q2s, q2r, scs, scr,
+    o2s, o2r, o3s, o3r, g1s, g1r, ghs, ghr, gvos, gvor,
 ):
     XN, YQ = R // 2, YH // 2
     N = Z * 2 * B
     L = N // 2
     features = R * F
+    F2 = F // 2
+    ZH = Z // 2
+    lo, hi = pl.ds(0, F2), pl.ds(F2, F2)
     r = lax.axis_index("row")
     c = lax.axis_index("col")
     d = lax.axis_index("depth")
@@ -96,9 +101,6 @@
 
     def span(index, size):
         return pl.ds(pl.multiple_of(index * size, size), size)
-
-    def block(depth, s):
-        return pl.ds(pl.multiple_of(depth * (2 * B) + s * B, B), B)
 
     def loop(count, body, start=0):
         def step(k, carry):
@@ -147,87 +149,146 @@
             near.append(Z - k)
 
     class Gather:
-        def __init__(self, src, buf, s1, r1, s2, r2, s3, r3):
-            self.src, self.buf = src, buf
-            self.sems = (s1, r1, s2, r2, s3, r3)
-
-        def first(self, j):
-            s1, r1 = self.sems[:2]
+        def __init__(self, src, buf, zb, *sems):
+            self.src, self.buf, self.zb = src, buf, zb
+            (self.ays, self.ayr, self.azs, self.azr, self.ass, self.asr,
+             self.bzs, self.bzr, self.bys, self.byr, self.bss, self.bsr) = sems
+
+        def ay_copy(self, j):
             return copy(
-                self.src, self.buf.at[core, mloc, block(d, yl)],
-                s1.at[j], r1.at[yl * YQ + mloc], reader(j),
+                self.src.at[:, lo], self.buf.at[core, mloc, d, yl, :, lo],
+                self.ays.at[j], self.ayr.at[yl * YQ + mloc], reader(j),
             )
 
-        def first_arrival(self, s, m):
-            s1, r1 = self.sems[:2]
+        def ay_arrival(self, s, m):
             return copy(
-                self.src, self.buf.at[core, m, block(d, s)],
-                s1.at[0], r1.at[s * YQ + m], owner(s, m),
+                self.src.at[:, lo], self.buf.at[core, m, d, s, :, lo],
+                self.ays.at[0], self.ayr.at[s * YQ + m], owner(s, m),
             )
 
+        def az_copy(self, k):
+            part = self.buf.at[core, :, d, :, :, lo]
+            return copy(
+                part, part, self.azs.at[k], self.azr.at[k], depth_device(depth_peer(k))
+            )
+
+        def az_arrival(self, k):
+            q = depth_peer(Z - k)
+            part = self.buf.at[core, :, q, :, :, lo]
+            return copy(part, part, self.azs.at[k], self.azr.at[k], depth_device(q))
+
+        def as_copy(self, k):
+            part = self.buf.at[core, :, depth_peer(Z - k), :, :, lo]
+            return copy(part, part, self.ass.at[k], self.asr.at[k], sibling)
+
+        def as_arrival(self, k):
+            part = self.buf.at[1 - core, :, depth_peer(Z - k), :, :, lo]
+            return copy(part, part, self.ass.at[k], self.asr.at[k], sibling)
+
+        def bz_copy(self, k):
+            return copy(
+                self.src.at[:, hi], self.zb.at[d], self.bzs.at[k], self.bzr.at[k],
+                depth_device(depth_peer(k)),
+            )
+
+        def bz_arrival(self, k):
+            q = depth_peer(Z - k)
+            return copy(
+                self.src.at[:, hi], self.zb.at[q], self.bzs.at[k], self.bzr.at[k],
+                depth_device(q),
+            )
+
+        def by_copy(self, j):
+            return copy(
+                self.zb, self.buf.at[core, mloc, :, yl, :, hi],
+                self.bys.at[j], self.byr.at[yl * YQ + mloc], reader(j),
+            )
+
+        def by_arrival(self, s, m):
+            return copy(
+                self.zb, self.buf.at[core, m, :, s, :, hi],
+                self.bys.at[0], self.byr.at[s * YQ + m], owner(s, m),
+            )
+
+        def bs_copy(self, s, m):
+            part = self.buf.at[core, m, :, s, :, hi]
+            i = s * YQ + m
+            return copy(part, part, self.bss.at[i], self.bsr.at[i], sibling)
+
+        def bs_arrival(self, s, m):
+            part = self.buf.at[1 - core, m, :, s, :, hi]
+            i = s * YQ + m
+            return copy(part, part, self.bss.at[i], self.bsr.at[i], sibling)
+
         def start(self):
+            for k in reversed(near):
+                self.bz_copy(k).start()
             for j in range(YH):
                 @pl.when(home & (yh == j))
                 def _():
-                    self.buf[core, mloc, block(d, yl)] = self.src[...]
+                    self.buf[core, mloc, d, yl, :, 0:F2] = self.src[:, 0:F2]
 
                 @pl.when(jnp.logical_not(home & (yh == j)))
                 def _():
-                    self.first(j).start()
-
-        def piece(self, which, q):
-            return self.buf.at[which, :, span(q, 2 * B)]
-
-        def z_copy(self, k):
-            part = self.piece(core, d)
-            return copy(
-                part, part, self.sems[2].at[k], self.sems[3].at[k],
-                depth_device(depth_peer(k)),
-            )
-
-        def z_arrival(self, k):
-            q = depth_peer(Z - k)
-            part = self.piece(core, q)
-            return copy(part, part, self.sems[2].at[k], self.sems[3].at[k], depth_device(q))
-
-        def s_copy(self, k):
-            part = self.piece(core, depth_peer(Z - k))
-            return copy(part, part, self.sems[4].at[k], self.sems[5].at[k], sibling)
-
-        def s_arrival(self, k):
-            part = self.piece(1 - core, depth_peer(Z - k))
-            return copy(part, part, self.sems[4].at[k], self.sems[5].at[k], sibling)
+                    self.ay_copy(j).start()
+            self.zb[d] = self.src[:, F2:F]
 
         def spread(self):
             for s in range(2):
                 for m in range(YQ):
                     @pl.when(jnp.logical_not(is_owner(s, m)))
                     def _():
-                        self.first_arrival(s, m).wait_recv()
+                        self.ay_arrival(s, m).wait_recv()
+            for k in reversed(near):
+                self.az_copy(k).start()
+            self.as_copy(0).start()
             for k in near:
-                self.z_copy(k).start()
-            self.s_copy(0).start()
-
-        def pass_on(self):
-            for k in near:
-                self.z_arrival(k).wait_recv()
-                self.s_copy(k).start()
+                self.bz_arrival(k).wait_recv()
+            for j in range(YH):
+                @pl.when(home & (yh == j))
+                def _():
+                    self.buf[core, mloc, :, yl, :, F2:F] = self.zb[...]
+
+                @pl.when(jnp.logical_not(home & (yh == j)))
+                def _():
+                    self.by_copy(j).start()
+
+        def pass_on(self, ks):
+            for k in ks:
+                self.az_arrival(k).wait_recv()
+                self.as_copy(k).start()
+
+        def pass_on_upper(self):
+            for s in range(2):
+                for m in range(YQ):
+                    @pl.when(jnp.logical_not(is_owner(s, m)))
+                    def _():
+                        self.by_arrival(s, m).wait_recv()
+                    self.bs_copy(s, m).start()
 
         def arrived(self):
             for k in [0] + near:
-                self.s_arrival(k).wait_recv()
+                self.as_arrival(k).wait_recv()
+            for s in range(2):
+                for m in range(YQ):
+                    self.bs_arrival(s, m).wait_recv()
 
         def drain(self):
             for j in range(YH):
                 @pl.when(jnp.logical_not(home & (yh == j)))
                 def _():
-                    self.first(j).wait_send()
+                    self.ay_copy(j).wait_send()
+                    self.by_copy(j).wait_send()
             for k in range(1, Z):
-                self.z_copy(k).wait_send()
+                self.az_copy(k).wait_send()
+                self.bz_copy(k).wait_send()
             for k in range(Z):
-                self.s_copy(k).wait_send()
-
-    gx = Gather(x_ref, xbuf, x1s, x1r, x2s, x2r, x3s, x3r)
+                self.as_copy(k).wait_send()
+            for s in range(2):
+                for m in range(YQ):
+                    self.bs_copy(s, m).wait_send()
+
+    gx = Gather(x_ref, xbuf, xzb, x1, x2, x3, x4, x5, x6, x7, x8, x9, x10, x11, x12)
     gx.start()
 
     def gv_copy(j):
@@ -262,12 +323,47 @@
         q = x_peer(XN - k)
         return copy(ref, buf.at[q], send.at[k], recv.at[k], x_device(q))
 
+    def w_onward(ref, buf, send, recv, k):
+        rows = ref.shape[0] // 2
+        part = buf.at[x_peer(XN - k), pl.ds(0 if k == 1 else rows, rows)]
+        return copy(part, part, send.at[k - 1], recv.at[k - 1], x_device(x_peer(k)))
+
+    def w_onward_arrival(ref, buf, send, recv, k):
+        rows = ref.shape[0] // 2
+        part = buf.at[x_peer(2), pl.ds(0 if k == 1 else rows, rows)]
+        return copy(part, part, send.at[k - 1], recv.at[k - 1], x_device(x_peer(XN - k)))
+
     gate_w = (wg_ref, wgbuf, wgs, wgr)
     up_w = (wu_ref, wubuf, wus, wur)
     down_w = (wd_ref, wdbuf, wds, wdr)
-    for k in range(1, XN):
-        w_copy(*gate_w, k).start()
-        w_copy(*up_w, k).start()
+    sides = (1,) if XN == 2 else (1, 3)
+
+    def w_start(*which):
+        for k in sides:
+            for w in which:
+                w_copy(*w, k).start()
+
+    def w_turn(*which):
+        for k in sides:
+            for w in which:
+                w_arrival(*w, k).wait_recv()
+                if XN == 4:
+                    w_onward(*w, k).start()
+
+    def w_finish(*which):
+        if XN == 4:
+            for k in sides:
+                for w in which:
+                    w_onward_arrival(*w, k).wait_recv()
+
+    def w_drain(*which):
+        for k in sides:
+            for w in which:
+                w_copy(*w, k).wait_send()
+                if XN == 4:
+                    w_onward(*w, k).wait_send()
+
+    w_start(gate_w, up_w)
 
     t1_copy = copy(tgt_ref, tg1, t1s, t1r, ypair)
     t1_copy.start()
@@ -295,19 +391,17 @@
     for k in range(1, Z):
         t2_copy(k).start()
 
-    gx.pass_on()
-
+    gx.pass_on(near[:5])
+    w_turn(gate_w, up_w)
+    w_start(down_w)
+    gx.pass_on(near[5:])
+    gx.pass_on_upper()
     for one in local_weights():
         one.wait()
-    for k in range(1, XN):
-        w_arrival(*gate_w, k).wait_recv()
-        w_arrival(*up_w, k).wait_recv()
-    for k in range(1, XN):
-        w_copy(*down_w, k).start()
 
     def gate_up(which, m):
         fl = 2 * m + which
-        wide = xbuf[which, m].astype(jnp.float32)
+        wide = xbuf[which, m].reshape(N, F).astype(jnp.float32)
         scaled = (wide * gvbuf[which, m, 0:1, :]).astype(jnp.bfloat16)
         ybuf[fl] = scaled
         acc[:, 0:H] += dot(scaled, wgbuf[fl])
@@ -318,7 +412,9 @@
 
     acc[...] = jnp.zeros_like(acc)
     st1send[...] = jnp.zeros_like(st1send)
+    w_finish(gate_w, up_w)
     loop(YQ, lambda m: gate_up(core, m))
+    w_turn(down_w)
     gb_arrival.wait_recv()
     gx.arrived()
     loop(YQ, lambda m: gate_up(1 - core, m))
@@ -343,13 +439,27 @@
             q1_copy(q).start()
     st1recv[r] = st1send[...]
 
+    near_half = span(core, L)
+    far_half = span(1 - core, L)
+
     def y2_copy(k):
         q = x_peer(k)
-        return copy(ybuf.at[q], y2buf.at[x], y2s.at[k], y2r.at[k], x_device(q))
+        return copy(
+            ybuf.at[q, near_half], y2buf.at[x, near_half], y2s.at[k], y2r.at[k], x_device(q)
+        )
 
     def y2_arrival(k):
         q = x_peer(XN - k)
-        return copy(ybuf.at[x], y2buf.at[q], y2s.at[k], y2r.at[k], x_device(q))
+        part = y2buf.at[q, near_half]
+        return copy(part, part, y2s.at[k], y2r.at[k], x_device(q))
+
+    def yb_copy(k):
+        part = y2buf.at[x_peer(XN - k), near_half]
+        return copy(part, part, ybs.at[k], ybr.at[k], sibling)
+
+    def yb_arrival(k):
+        part = y2buf.at[x_peer(XN - k), far_half]
+        return copy(part, part, ybs.at[k], ybr.at[k], sibling)
 
     for k in range(1, XN):
         y2_copy(k).start()
@@ -362,15 +472,10 @@
     rs_copy.wait_recv()
     total = (acc[span(yl, L)] + rsrecv[...].astype(jnp.float32)) * inv_norm
     gate, up = total[:, 0:H], total[:, H:2 * H]
-    hbuf[my_seat] = (gate * jax.nn.sigmoid(gate) * up).astype(jnp.bfloat16)
-
-    def h_copy(q):
-        part = hbuf.at[my_seat]
-        return copy(part, part, hs.at[q], hr.at[r], row_device(q))
-
-    def h_arrival(q):
-        part = hbuf.at[seat(q)]
-        return copy(part, part, hs.at[q], hr.at[q], row_device(q))
+    hbuf[yl] = (gate * jax.nn.sigmoid(gate) * up).astype(jnp.bfloat16)
+
+    h_copy = copy(hbuf.at[yl], hbuf.at[yl], hs, hr, ypair)
+    h_arrival = copy(hbuf.at[1 - yl], hbuf.at[1 - yl], hs, hr, ypair)
 
     def gu_copy(q):
         part = gubuf.at[my_seat]
@@ -380,11 +485,10 @@
         part = gubuf.at[seat(q)]
         return copy(part, part, gus.at[q], gur.at[q], row_device(q))
 
-    h_copy(pair_row).start()
+    h_copy.start()
     gubuf[my_seat] = total.astype(jnp.bfloat16)
 
-    for k in range(1, XN):
-        w_arrival(*down_w, k).wait_recv()
+    w_finish(down_w)
 
     def ob_copy(s):
         part = pl.ds(pl.multiple_of(s * L, L), L)
@@ -392,7 +496,7 @@
 
     def down(s):
         rows = span(s, L)
-        act = hbuf[x * 2 + s]
+        act = hbuf[s]
         for m in range(YQ):
             osend[m, rows] = dot(act, wdbuf[2 * m + 1 - core]).astype(jnp.bfloat16)
         ob_copy(s).start()
@@ -401,21 +505,26 @@
 
     down(yl)
     for k in range(1, R):
-        q = row_peer(k)
-
-        @pl.when(q != pair_row)
-        def _():
-            h_copy(q).start()
-        gu_copy(q).start()
-
-    def oz_copy(q):
+        gu_copy(row_peer(k)).start()
+
+    def za_copy(q):
         return copy(
-            zsend.at[:, span(q, 2 * B)], zrecv.at[d], ozs.at[q], ozr.at[d], depth_device(q)
-        )
-
-    def oz_arrival(q):
+            zsend.at[:, q, :, :, lo], zra.at[d], zas.at[q], zar.at[d], depth_device(q)
+        )
+
+    def za_arrival(q):
         return copy(
-            zsend.at[:, span(q, 2 * B)], zrecv.at[q], ozs.at[q], ozr.at[q], depth_device(q)
+            zsend.at[:, q, :, :, lo], zra.at[q], zas.at[q], zar.at[q], depth_device(q)
+        )
+
+    def yb2_copy(s, m):
+        return copy(
+            zsend.at[m, :, s, :, hi], yrb.at[yh], ybbs.at[s * YQ + m], ybbr.at[yh], owner(s, m)
+        )
+
+    def yb2_arrival(j):
+        return copy(
+            zsend.at[0, :, 0, :, hi], yrb.at[j], ybbs.at[0], ybbr.at[j], reader(j)
         )
 
     def pair_sum(s):
@@ -424,75 +533,100 @@
         for m in range(YQ):
             both = oown[m, rows] + osib[m, rows].astype(jnp.float32)
             oown[m, rows] = both
-            zsend[m, rows] = both.astype(jnp.bfloat16)
+            zsend[m, pl.ds(s * ZH, ZH)] = both.astype(jnp.bfloat16).reshape(ZH, 2, B, F)
         for i in range(Z // 2):
             q = s * (Z // 2) + rem(d + i, Z // 2)
 
             @pl.when(q != d)
             def _():
-                oz_copy(q).start()
+                za_copy(q).start()
 
     pair_sum(yl)
-    h_arrival(pair_row).wait_recv()
+    h_arrival.wait_recv()
     down(1 - yl)
     pair_sum(1 - yl)
-
-    y2buf[x] = ybuf[x]
-    y2t[:, span(x, N)] = ybuf[x].T
-    for k in range(1, XN):
-        q = x_peer(XN - k)
-        y2_arrival(k).wait_recv()
-        y2t[:, span(q, N)] = y2buf[q].T
-
-    mine = span(d, 2 * B)
-    for k in near:
-        q = depth_peer(k)
-        oz_arrival(q).wait_recv()
-        for m in range(YQ):
-            oown[m, mine] += zrecv[q, m].astype(jnp.float32)
-    for m in range(YQ):
-        ysend[m] = oown[m, mine].astype(jnp.bfloat16)
-
-    def oy_copy(s, m):
-        return copy(
-            ysend.at[m, pl.ds(s * B, B)], yrecv.at[yh], oys.at[s * YQ + m], oyr.at[yh],
-            owner(s, m),
-        )
-
-    def oy_arrival(j):
-        return copy(ysend.at[0, pl.ds(0, B)], yrecv.at[j], oys.at[0], oyr.at[j], reader(j))
 
     for s in range(2):
         for m in range(YQ):
             @pl.when(is_owner(s, m))
             def _():
-                yrecv[yh] = ysend[m, s * B:(s + 1) * B]
+                yrb[yh] = zsend[m, :, s, :, F2:F]
 
             @pl.when(jnp.logical_not(is_owner(s, m)))
             def _():
-                oy_copy(s, m).start()
-    output = x_ref[...].astype(jnp.float32)
+                yb2_copy(s, m).start()
+
+    y2t[:, span(x, N)] = ybuf[x].T
+
+    mine = span(d, 2 * B)
+    for k in near:
+        q = depth_peer(k)
+        za_arrival(q).wait_recv()
+        for m in range(YQ):
+            oown[m, mine, 0:F2] += zra[q, m].reshape(2 * B, F2).astype(jnp.float32)
+    for m in range(YQ):
+        ysa[m] = oown[m, mine, 0:F2].astype(jnp.bfloat16).reshape(2, B, F2)
+
+    def ya_copy(s, m):
+        return copy(
+            ysa.at[m, s], yra.at[yh], yas.at[s * YQ + m], yar.at[yh], owner(s, m)
+        )
+
+    def ya_arrival(j):
+        return copy(ysa.at[0, 0], yra.at[j], yas.at[0], yar.at[j], reader(j))
+
+    for s in range(2):
+        for m in range(YQ):
+            @pl.when(is_owner(s, m))
+            def _():
+                yra[yh] = ysa[m, s]
+
+            @pl.when(jnp.logical_not(is_owner(s, m)))
+            def _():
+                ya_copy(s, m).start()
+
+    upper = jnp.zeros((Z, B, F2), jnp.float32)
     for j in range(YH):
         @pl.when(jnp.logical_not(home & (yh == j)))
         def _():
-            oy_arrival(j).wait_recv()
-        output = output + yrecv[j].astype(jnp.float32)
-    outblk[...] = output.astype(jnp.bfloat16)
-
-    ga = Gather(outblk, obuf, a1s, a1r, a2s, a2r, a3s, a3r)
+            yb2_arrival(j).wait_recv()
+        upper = upper + yrb[j].astype(jnp.float32)
+    zsb[...] = upper.astype(jnp.bfloat16)
+
+    def zb2_copy(q):
+        return copy(zsb.at[q], zrb.at[d], zbs.at[q], zbr.at[d], depth_device(q))
+
+    def zb2_arrival(q):
+        return copy(zsb.at[q], zrb.at[q], zbs.at[q], zbr.at[q], depth_device(q))
+
+    for k in reversed(near):
+        zb2_copy(depth_peer(k)).start()
+
+    for k in range(1, XN):
+        y2_arrival(k).wait_recv()
+        yb_copy(k).start()
+
+    output = x_ref[:, 0:F2].astype(jnp.float32)
+    for j in range(YH):
+        @pl.when(jnp.logical_not(home & (yh == j)))
+        def _():
+            ya_arrival(j).wait_recv()
+        output = output + yra[j].astype(jnp.float32)
+    outblk[:, 0:F2] = output.astype(jnp.bfloat16)
+    output = x_ref[:, F2:F].astype(jnp.float32) + zsb[d].astype(jnp.float32)
+    for k in near:
+        q = depth_peer(k)
+        zb2_arrival(q).wait_recv()
+        output = output + zrb[q].astype(jnp.float32)
+    outblk[:, F2:F] = output.astype(jnp.bfloat16)
+
+    ga = Gather(outblk, obuf, ozb, a1, a2, a3, a4, a5, a6, a7, a8, a9, a10, a11, a12)
     ga.start()
 
-    ht[:, span(my_seat, L)] = hbuf[my_seat].T
-
-    def hidden_step(k):
-        q = row_peer(k)
-
-        @pl.when(q != pair_row)
-        def _():
-            h_arrival(q).wait_recv()
-        ht[:, span(seat(q), L)] = hbuf[seat(q)].T
-
-    loop(R, hidden_step, 1)
+    for k in range(1, XN):
+        q = x_peer(XN - k)
+        yb_arrival(k).wait_recv()
+        y2t[:, span(q, N)] = y2buf[q].T
 
     ga.spread()
 
@@ -507,7 +641,9 @@
         gate, up = both[:, 0:H], both[:, H:2 * H]
         sig = jax.nn.sigmoid(gate)
         coef[s, :, 0:H] = inv * (up * sig * (1.0 + gate * (1.0 - sig)))
-        coef[s, :, H:2 * H] = inv * (gate * sig)
+        swish = gate * sig
+        coef[s, :, H:2 * H] = inv * swish
+        ht[:, span(s, L)] = (swish * up).astype(jnp.bfloat16).T
 
     for k in range(1, R):
         q = row_peer(k)
@@ -524,7 +660,8 @@
     loop(R, coef_step, 1)
     coef_of(r)
 
-    ga.pass_on()
+    ga.pass_on(near)
+    ga.pass_on_upper()
 
     target = tgsend[...]
     for k in range(1, Z):
@@ -532,7 +669,7 @@
         target = target + tg2[depth_peer(Z - k)]
 
     def stats(which, m):
-        wide = obuf[which, m].astype(jnp.float32)
+        wide = obuf[which, m].reshape(N, F).astype(jnp.float32)
         head = gvbuf[which, m, 1:2, :]
         squares = jnp.sum(wide * wide, axis=1, keepdims=True)
         products = jnp.sum(wide * head, axis=1, keepdims=True)
@@ -547,6 +684,29 @@
     loop(YQ, lambda m: stats(1 - core, m))
     q2_copy = copy(st2send, st2recv, q2s, q2r, ypair)
     q2_copy.start()
+
+    def o2_copy(k):
+        q = x_peer(k)
+        part = obuf.at[rem(q, 2), lax.div(q, jnp.int32(2)), pl.ds(core * ZH, ZH)]
+        return copy(
+            part, o2buf.at[x, pl.ds(core * ZH, ZH)], o2s.at[k], o2r.at[k], x_device(q)
+        )
+
+    def o2_arrival(k):
+        q = x_peer(XN - k)
+        part = o2buf.at[q, pl.ds(core * ZH, ZH)]
+        return copy(part, part, o2s.at[k], o2r.at[k], x_device(q))
+
+    def o3_copy(k):
+        part = o2buf.at[x_peer(XN - k), pl.ds(core * ZH, ZH)]
+        return copy(part, part, o3s.at[k], o3r.at[k], sibling)
+
+    def o3_arrival(k):
+        part = o2buf.at[x_peer(XN - k), pl.ds((1 - core) * ZH, ZH)]
+        return copy(part, part, o3s.at[k], o3r.at[k], sibling)
+
+    for k in range(1, XN):
+        o2_copy(k).start()
     q2_copy.wait_recv()
     sums = st2send[...] + st2recv[...]
     inv_final = lax.rsqrt(sums[0:2] / features + norm_eps)
@@ -555,16 +715,25 @@
     slope = jnp.clip(values - target[0:2], -huber_delta, huber_delta)
     scale_lanes = inv_final * slope
     shrink_lanes = inv_final * inv_final * (slope * values / features)
-    scale = jnp.concatenate([to_column(scale_lanes[s:s + 1]) for s in range(2)], axis=0)
-    shrink = jnp.concatenate([to_column(shrink_lanes[s:s + 1]) for s in range(2)], axis=0)
-
-    def go_copy(k):
-        q = x_peer(k)
-        return copy(gobuf.at[q], go2buf.at[x], gos.at[k], gor.at[k], x_device(q))
-
-    def go_arrival(k):
+    scsend[...] = jnp.concatenate([scale_lanes, shrink_lanes] * 2, axis=0)
+
+    def sc_copy(k):
+        return copy(scsend, screcv.at[x], scs.at[k], scr.at[k], x_device(x_peer(k)))
+
+    def sc_arrival(k):
         q = x_peer(XN - k)
-        return copy(gobuf.at[x], go2buf.at[q], gos.at[k], gor.at[k], x_device(q))
+        return copy(scsend, screcv.at[q], scs.at[k], scr.at[k], x_device(q))
+
+    for k in range(1, XN):
+        sc_copy(k).start()
+
+    def columns(lanes):
+        return (
+            jnp.concatenate([to_column(lanes[0:1]), to_column(lanes[1:2])], axis=0),
+            jnp.concatenate([to_column(lanes[2:3]), to_column(lanes[3:4])], axis=0),
+        )
+
+    scale, shrink = columns(scsend[...])
 
     gsum[...] = jnp.zeros_like(gsum)
     ghpart[...] = jnp.zeros_like(ghpart)
@@ -572,7 +741,7 @@
     def grad_output(fl):
         which = rem(fl, 2)
         m = lax.div(fl, jnp.int32(2))
-        wide = obuf[which, m].astype(jnp.float32)
+        wide = obuf[which, m].reshape(N, F).astype(jnp.float32)
         head = gvbuf[which, m, 1:2, :]
         gobuf[fl] = (scale * head - shrink * wide).astype(jnp.bfloat16)
         gsum[pl.ds(fl, 1), :] = jnp.sum(wide * scale, axis=0, keepdims=True)
@@ -583,8 +752,6 @@
     g1_copy = copy(ghsend, ghrecv, g1s, g1r, ypair)
     ghsend[...] = ghpart[span(1 - yl, L)].astype(jnp.bfloat16)
     g1_copy.start()
-    for k in range(1, XN):
-        go_copy(k).start()
 
     def gvo_copy(q):
         return copy(gsum, grecv.at[r], gvos.at[q], gvor.at[r], row_device(q))
@@ -600,7 +767,6 @@
         part = ghbuf.at[seat(q)]
         return copy(part, part, ghs.at[q], ghr.at[q], row_device(q))
 
-    go2buf[x] = gobuf[x]
     g1_copy.wait_recv()
     ghbuf[my_seat] = (
         ghpart[span(yl, L)] + ghrecv[...].astype(jnp.float32)
@@ -611,8 +777,18 @@
         gvo_copy(row_peer(k)).start()
     grecv[r] = gsum[...]
 
+    go2buf[x] = gobuf[x]
     for k in range(1, XN):
-        go_arrival(k).wait_recv()
+        o2_arrival(k).wait_recv()
+        o3_copy(k).start()
+    head = gvbuf[rem(x, 2), lax.div(x, jnp.int32(2)), 1:2, :]
+    for k in range(1, XN):
+        q = x_peer(XN - k)
+        sc_arrival(k).wait_recv()
+        o3_arrival(k).wait_recv()
+        scale, shrink = columns(screcv[q])
+        wide = o2buf[q].reshape(N, F).astype(jnp.float32)
+        go2buf[q] = (scale * head - shrink * wide).astype(jnp.bfloat16)
     tokens = XN * N
     tile = min(128, H)
 
@@ -668,19 +844,21 @@
     q2_copy.wait_send()
     g1_copy.wait_send()
 
+    w_drain(gate_w, up_w, down_w)
+    h_copy.wait_send()
+
     def x_sends(k):
-        w_copy(*gate_w, k).wait_send()
-        w_copy(*up_w, k).wait_send()
-        w_copy(*down_w, k).wait_send()
         y2_copy(k).wait_send()
-        go_copy(k).wait_send()
+        yb_copy(k).wait_send()
+        o2_copy(k).wait_send()
+        o3_copy(k).wait_send()
+        sc_copy(k).wait_send()
 
     loop(XN, x_sends, 1)
 
     def row_sends(k):
         q = row_peer(k)
         q1_copy(q).wait_send()
-        h_copy(q).wait_send()
         gu_copy(q).wait_send()
         gh_copy(q).wait_send()
         gvo_copy(q).wait_send()
@@ -689,7 +867,8 @@
 
     def depth_sends(k):
         t2_copy(k).wait_send()
-        oz_copy(depth_peer(k)).wait_send()
+        za_copy(depth_peer(k)).wait_send()
+        zb2_copy(depth_peer(k)).wait_send()
 
     loop(Z, depth_sends, 1)
     for s in range(2):
@@ -697,7 +876,8 @@
         for m in range(YQ):
             @pl.when(jnp.logical_not(is_owner(s, m)))
             def _():
-                oy_copy(s, m).wait_send()
+                ya_copy(s, m).wait_send()
+                yb2_copy(s, m).wait_send()
 
 
 def build(mesh):
@@ -722,26 +902,37 @@
         bf, f32 = jnp.bfloat16, jnp.float32
         V = pltpu.VMEM
         dma = lambda *shape: pltpu.SemaphoreType.DMA(shape)
+        F2 = F // 2
+        gather = [
+            dma(YH), dma(2 * YQ), dma(Z), dma(Z), dma(Z), dma(Z),
+            dma(Z), dma(Z), dma(YH), dma(2 * YQ), dma(2 * YQ), dma(2 * YQ),
+        ]
         scratch = [
-            V((2, YQ, N, F), bf), V((XN, N, F), bf), V((XN, N, F), bf), V((F, XN * N), bf),
+            V((2, YQ, Z, 2, B, F), bf), V((Z, B, F2), bf),
+            V((XN, N, F), bf), V((XN, N, F), bf), V((F, XN * N), bf),
             V((XN, F, H), bf), V((XN, F, H), bf), V((XN, H, F), bf),
             V((2, YQ, 8, F), f32), V((8, L), f32), V((8, L), f32), V((Z, 8, L), f32),
             V((N, 2 * H), f32), V((L, 2 * H), bf), V((L, 2 * H), bf),
             V((8, L), f32), V((R, 8, L), f32),
-            V((R, L, H), bf), V((H, R * L), bf), V((R, L, 2 * H), bf), V((R, L, 2 * H), f32),
+            V((2, L, H), bf), V((H, R * L), bf), V((R, L, 2 * H), bf), V((R, L, 2 * H), f32),
             V((YQ, N, F), bf), V((YQ, N, F), bf), V((YQ, N, F), f32),
-            V((YQ, N, F), bf), V((Z, YQ, 2 * B, F), bf), V((YQ, 2 * B, F), bf), V((YH, B, F), bf),
-            V((B, F), bf), V((2, YQ, N, F), bf),
-            V((8, L), f32), V((8, L), f32),
-            V((XN, N, F), bf), V((XN, N, F), bf), V((N, H), f32), V((L, H), bf), V((L, H), bf),
+            V((YQ, Z, 2, B, F), bf), V((Z, YQ, 2, B, F2), bf), V((YH, B, F2), bf),
+            V((YH, Z, B, F2), bf), V((Z, B, F2), bf), V((YQ, 2, B, F2), bf), V((Z, B, F2), bf),
+            V((B, F), bf), V((2, YQ, Z, 2, B, F), bf), V((Z, B, F2), bf),
+            V((8, L), f32), V((8, L), f32), V((8, L), f32), V((XN, 8, L), f32),
+            V((XN, Z, 2, B, F), bf), V((XN, N, F), bf), V((XN, N, F), bf),
+            V((N, H), f32), V((L, H), bf), V((L, H), bf),
             V((R, L, H), bf), V((R, L, 2 * H), bf), V((8, F), f32), V((R, 8, F), f32),
-            dma(YH), dma(2 * YQ), dma(Z), dma(Z), dma(Z), dma(Z),
+            *gather,
             dma(YH), dma(YQ), dma(), dma(), dma(), dma(), dma(Z), dma(Z),
-            dma(3), dma(XN), dma(XN), dma(XN), dma(XN), dma(XN), dma(XN),
-            dma(R), dma(R), dma(), dma(), dma(XN), dma(XN), dma(R), dma(R), dma(R), dma(R),
-            dma(2), dma(2), dma(Z), dma(Z), dma(2 * YQ), dma(YH),
-            dma(YH), dma(2 * YQ), dma(Z), dma(Z), dma(Z), dma(Z), dma(), dma(),
-            dma(XN), dma(XN), dma(), dma(), dma(R), dma(R), dma(R), dma(R),
+            dma(3), dma(4), dma(4), dma(4), dma(4), dma(4), dma(4),
+            dma(R), dma(R), dma(), dma(), dma(XN), dma(XN), dma(XN), dma(XN),
+            dma(), dma(), dma(R), dma(R),
+            dma(2), dma(2), dma(Z), dma(Z), dma(2 * YQ), dma(YH), dma(2 * YQ), dma(YH),
+            dma(Z), dma(Z),
+            *gather,
+            dma(), dma(), dma(XN), dma(XN), dma(XN), dma(XN), dma(XN), dma(XN),
+            dma(), dma(), dma(R), dma(R), dma(R), dma(R),
         ]
         vmem = pl.BlockSpec(memory_space=pltpu.VMEM)
         hbm = pl.BlockSpec(memory_space=pl.ANY)

time: 133 us -> 115 us (0.86)
  Pallas kernels: 125 us -> 107 us
    pallas_call x1, Pallas kernels: 125 us -> 107 us  [per_device(): pl.pallas_call(functools.partial(kernel, R, YH, Z, B, F, H), out_shape=(j...]
where the time goes in v3:
time: 115 us; the launch traced here: 114 us
  Pallas kernels  107 us (93%)
  local copies, waits for them, and re-layouts  6.61 us (6%)
    pallas_call x1, Pallas kernels, per_device(): pl.pallas_call(functools.partial(kernel, R, YH, Z, B, F, H), out_shape=(j...  107 us
    unnamed x19, local copies, waits for them, and re-layouts  4.56 us

profile of v3, /device:TPU:1, one launch (start us, length us, event | category | flops | bytes accessed | tf_op | source)
XLA Modules:
  0.0 114.0 jit_solution(7647367829226330138)
XLA Ops:
  0.6 0.0 copy-start
  0.7 0.0 copy-start.7
  0.7 0.6 copy-done.7
  1.4 0.2 copy-done
  1.5 0.0 copy-start.5
  1.5 0.0 copy-start.1
  1.5 0.0 copy-start.2
  1.5 0.7 gather_fusion
  2.2 0.0 copy-start.4
  2.2 0.2 dynamic_update_slice.3.tgt_ref
  2.4 0.0 copy-done.5
  2.4 0.0 copy-start.6
  2.5 0.7 copy-done.6
  3.2 0.0 copy-done.1
  3.2 0.0 copy-done.2
  3.2 0.0 copy-done.4
  3.2 0.0 copy-start.3
  3.2 0.9 copy-done.3
  4.1 106.6 %shard_map.119 = (bf16[512,256]{1,0:T(8,128)(2,1)S(1)}, bf16[512,256]{1,0:T(8,128)(2,1)S(1)}, bf16[256,512]{1,0:T(8,128)(2,1)S(1)}, f32[8,128]{1,0:T(8,128)S(1)}, f32[8,512]{1,0:T(8,128)S(1)}) custom-call(bf16[16,512]{1,0:T(8,128)(2,1)S(1)} %copy-done.4, f32[8,512]{1,0:T(8,128)S(1)} %scatter.9.gv_ref, f32[8,128]{1,0:T(8,128)S(1)} %dynamic_update_slice.3.tgt_ref, ...), custom_call_target="tpu_custom_call" | custom-call | tf_op jit(solution)/shard_map/pallas_call | solution.py:939
  110.7 0.6 dynamic-slice_bitcast_fusion
  111.3 0.6 slice.32
  111.9 0.7 copy.18
  112.6 0.7 copy.19
  113.3 0.7 copy.20
  (6 shorter events, 0.1 us)
Async XLA Ops:
  0.6 0.9 copy-start
  0.7 0.7 copy-start.7
  1.5 0.9 copy-start.5
  1.5 1.6 %copy-start.1 = (bf16[512,256]{1,0:T(8,128)(2,1)S(1)}, bf16[512,256]{1,0:T(8,128)(2,1)}, u32[]{:S(2)}) copy-start(bf16[512,256]{1,0:T(8,128)(2,1)} %wg_ref.1) | copy-start | bytes 786436
  1.5 1.6 %copy-start.2 = (bf16[512,256]{1,0:T(8,128)(2,1)S(1)}, bf16[512,256]{1,0:T(8,128)(2,1)}, u32[]{:S(2)}) copy-start(bf16[512,256]{1,0:T(8,128)(2,1)} %wu_ref.1) | copy-start | bytes 786436
  2.2 1.0 copy-start.4
  2.4 0.7 copy-start.6
  3.2 1.0 copy-start.3

commit v4 on v3

--- a/solution.py
+++ b/solution.py
@@ -10,6 +10,7 @@
 MESH = pl.DeviceIdType.MESH
 norm_eps = 1e-06
 huber_delta = 1.0
+VMEM_MB = 56
 
 
 def rem(value, size):
@@ -28,15 +29,16 @@
 
 def kernel(
     R, YH, Z, B, F, H,
-    x_ref, gv_ref, tgt_ref, wg_ref, wu_ref, wd_ref,
+    x_ref, gain_ref, head_ref, index_ref, table_ref, wg_ref, wu_ref, wd_ref,
     dg_ref, du_ref, dd_ref, val_ref, gval_ref,
-    xbuf, xzb, ybuf, y2buf, y2t, wgbuf, wubuf, wdbuf, gvbuf, tg1, tgsend, tg2,
-    acc, rssend, rsrecv, st1send, st1recv, hbuf, ht, gubuf, coef,
+    xbuf, xzb, ybuf, y2buf, y2t, wgbuf, wubuf, wdbuf, gnbuf, hdbuf, xblk, index, table,
+    tgown, tg1, tgsend, tg2,
+    acc, stat, rssend, rsrecv, st1send, st1recv, hbuf, ht, gubuf, coef,
     osend, osib, oown, zsend, zra, yra, yrb, zrb, ysa, zsb, outblk, obuf, ozb,
     st2send, st2recv, scsend, screcv, o2buf, gobuf, go2buf,
     ghpart, ghsend, ghrecv, ghbuf, ggbuf, gsum, grecv,
-    x1, x2, x3, x4, x5, x6, x7, x8, x9, x10, x11, x12, gvs, gvr, gbs, gbr, t1s, t1r, t2s, t2r,
-    wls, wgs, wgr, wus, wur, wds, wdr, q1s, q1r, rss, rsr, y2s, y2r, ybs, ybr, hs, hr, gus, gur,
+    x1, x2, x3, x4, x5, x6, x7, x8, x9, x10, x11, x12, gvs, gvr, hds, hdr, gbs, gbr, los, t1s, t1r, t2s, t2r,
+    wls, wgs, wgr, wus, wur, wds, wdr, q1s, q1r, rss, rsr, y2s, y2r, ybs, ybr, hs, hr, gps, gpr, gus, gur,
     obs, obr, zas, zar, yas, yar, ybbs, ybbr, zbs, zbr,
     a1, a2, a3, a4, a5, a6, a7, a8, a9, a10, a11, a12, q2s, q2r, scs, scr,
     o2s, o2r, o3s, o3r, g1s, g1r, ghs, ghr, gvos, gvor,
@@ -119,6 +121,12 @@
     def to_column(lanes):
         return jnp.sum(jnp.where(eye, lanes, 0.0), axis=1, keepdims=True)
 
+    local_x = pltpu.make_async_copy(x_ref, xblk, los.at[0])
+    local_index = pltpu.make_async_copy(index_ref, index, los.at[1])
+    local_table = pltpu.make_async_copy(table_ref, table, los.at[2])
+    for one in (local_x, local_index, local_table):
+        one.start()
+
     barrier = pltpu.get_barrier_semaphore()
 
     def greet(device):
@@ -149,8 +157,8 @@
             near.append(Z - k)
 
     class Gather:
-        def __init__(self, src, buf, zb, *sems):
-            self.src, self.buf, self.zb = src, buf, zb
+        def __init__(self, src, local, buf, zb, *sems):
+            self.src, self.local, self.buf, self.zb = src, local, buf, zb
             (self.ays, self.ayr, self.azs, self.azr, self.ass, self.asr,
              self.bzs, self.bzr, self.bys, self.byr, self.bss, self.bsr) = sems
 
@@ -221,17 +229,18 @@
             return copy(part, part, self.bss.at[i], self.bsr.at[i], sibling)
 
         def start(self):
-            for k in reversed(near):
-                self.bz_copy(k).start()
             for j in range(YH):
-                @pl.when(home & (yh == j))
-                def _():
-                    self.buf[core, mloc, d, yl, :, 0:F2] = self.src[:, 0:F2]
-
                 @pl.when(jnp.logical_not(home & (yh == j)))
                 def _():
                     self.ay_copy(j).start()
-            self.zb[d] = self.src[:, F2:F]
+            for k in reversed(near):
+                self.bz_copy(k).start()
+
+        def keep(self):
+            @pl.when(home)
+            def _():
+                self.buf[core, mloc, d, yl, :, 0:F2] = self.local[:, 0:F2]
+            self.zb[d] = self.local[:, F2:F]
 
         def spread(self):
             for s in range(2):
@@ -288,23 +297,34 @@
                 for m in range(YQ):
                     self.bs_copy(s, m).wait_send()
 
-    gx = Gather(x_ref, xbuf, xzb, x1, x2, x3, x4, x5, x6, x7, x8, x9, x10, x11, x12)
+    gx = Gather(x_ref, xblk, xbuf, xzb, x1, x2, x3, x4, x5, x6, x7, x8, x9, x10, x11, x12)
     gx.start()
 
-    def gv_copy(j):
-        return copy(gv_ref, gvbuf.at[core, mloc], gvs.at[j], gvr.at[mloc], reader(j))
-
-    def gv_arrival(m):
-        return copy(gv_ref, gvbuf.at[core, m], gvs.at[0], gvr.at[m], owner(0, m))
+    def gn_copy(j):
+        return copy(gain_ref, gnbuf.at[core, mloc], gvs.at[j], gvr.at[mloc], reader(j))
+
+    def hd_copy(j):
+        return copy(head_ref, hdbuf.at[core, mloc], hds.at[j], hdr.at[mloc], reader(j))
+
+    def gn_arrival(m):
+        return copy(gain_ref, gnbuf.at[core, m], gvs.at[0], gvr.at[m], owner(0, m))
+
+    def hd_arrival(m):
+        return copy(head_ref, hdbuf.at[core, m], hds.at[0], hdr.at[m], owner(0, m))
+
+    gn_local = pltpu.make_async_copy(gain_ref, gnbuf.at[core, mloc], los.at[3])
+    hd_local = pltpu.make_async_copy(head_ref, hdbuf.at[core, mloc], los.at[4])
+
+    @pl.when((yl == 0) & home)
+    def _():
+        gn_local.start()
+        hd_local.start()
 
     for j in range(YH):
-        @pl.when((yl == 0) & home & (yh == j))
-        def _():
-            gvbuf[core, mloc] = gv_ref[...]
-
         @pl.when((yl == 0) & jnp.logical_not(home & (yh == j)))
         def _():
-            gv_copy(j).start()
+            gn_copy(j).start()
+            hd_copy(j).start()
 
     def local_weights():
         return (
@@ -365,21 +385,54 @@
 
     w_start(gate_w, up_w)
 
-    t1_copy = copy(tgt_ref, tg1, t1s, t1r, ypair)
+    local_x.wait()
+    gx.keep()
+
+    local_index.wait()
+    local_table.wait()
+    place = d * (2 * B) + yl * B
+    place_row = lax.div(place, jnp.int32(L))
+    place_lane = rem(place, L)
+    table_lanes = lax.broadcasted_iota(jnp.int32, (1, 128), 1)
+    lanes = lax.broadcasted_iota(jnp.int32, (1, L), 1)
+
+    def look_up(i, found):
+        entry = index[0, i]
+        line = table[pl.ds(lax.div(entry, jnp.int32(128)), 1), :]
+        value = jnp.sum(
+            jnp.where(table_lanes == rem(entry, 128), line, 0.0), axis=1, keepdims=True
+        )
+        return found + jnp.where(lanes == place_lane + i, value, 0.0)
+
+    found = lax.fori_loop(0, B, look_up, jnp.zeros((1, L), jnp.float32))
+    tile_rows = lax.broadcasted_iota(jnp.int32, (8, L), 0)
+    tgown[...] = jnp.where(tile_rows == place_row, found, 0.0)
+    t1_copy = copy(tgown, tg1, t1s, t1r, ypair)
     t1_copy.start()
 
     gx.spread()
 
     for m in range(YQ):
-        @pl.when(jnp.logical_not((yl == 0) & is_owner(0, m)))
+        here = (yl == 0) & is_owner(0, m)
+
+        @pl.when(here)
         def _():
-            gv_arrival(m).wait_recv()
-    gb_copy = copy(gvbuf.at[core], gvbuf.at[core], gbs, gbr, sibling)
-    gb_arrival = copy(gvbuf.at[1 - core], gvbuf.at[1 - core], gbs, gbr, sibling)
+            gn_local.wait()
+            hd_local.wait()
+
+        @pl.when(jnp.logical_not(here))
+        def _():
+            gn_arrival(m).wait_recv()
+            hd_arrival(m).wait_recv()
+    gb_copy = copy(gnbuf.at[core], gnbuf.at[core], gbs.at[0], gbr.at[0], sibling)
+    hb_copy = copy(hdbuf.at[core], hdbuf.at[core], gbs.at[1], gbr.at[1], sibling)
+    gb_arrival = copy(gnbuf.at[1 - core], gnbuf.at[1 - core], gbs.at[0], gbr.at[0], sibling)
+    hb_arrival = copy(hdbuf.at[1 - core], hdbuf.at[1 - core], gbs.at[1], gbr.at[1], sibling)
     gb_copy.start()
+    hb_copy.start()
 
     t1_copy.wait_recv()
-    tgsend[...] = tgt_ref[...] + tg1[...]
+    tgsend[...] = tgown[...] + tg1[...]
 
     def t2_copy(k):
         return copy(tgsend, tg2.at[d], t2s.at[k], t2r.at[k], depth_device(depth_peer(k)))
@@ -391,27 +444,34 @@
     for k in range(1, Z):
         t2_copy(k).start()
 
-    gx.pass_on(near[:5])
     w_turn(gate_w, up_w)
     w_start(down_w)
-    gx.pass_on(near[5:])
+    gx.pass_on(near)
     gx.pass_on_upper()
     for one in local_weights():
         one.wait()
 
+    def fold(wide):
+        total = wide[:, 0:128]
+        for i in range(1, F // 128):
+            total = total + wide[:, 128 * i:128 * (i + 1)]
+        return total
+
+    def lane_sums(folded):
+        column = jnp.sum(folded, axis=1, keepdims=True)
+        return [to_lanes(column[s * L:(s + 1) * L]) for s in range(2)]
+
     def gate_up(which, m):
         fl = 2 * m + which
         wide = xbuf[which, m].reshape(N, F).astype(jnp.float32)
-        scaled = (wide * gvbuf[which, m, 0:1, :]).astype(jnp.bfloat16)
+        scaled = (wide * gnbuf[which, m]).astype(jnp.bfloat16)
         ybuf[fl] = scaled
         acc[:, 0:H] += dot(scaled, wgbuf[fl])
         acc[:, H:2 * H] += dot(scaled, wubuf[fl])
-        squares = jnp.sum(wide * wide, axis=1, keepdims=True)
-        for s in range(2):
-            st1send[s:s + 1, :] += to_lanes(squares[s * L:(s + 1) * L])
+        stat[0] += fold(wide * wide)
 
     acc[...] = jnp.zeros_like(acc)
-    st1send[...] = jnp.zeros_like(st1send)
+    stat[...] = jnp.zeros_like(stat)
     w_finish(gate_w, up_w)
     loop(YQ, lambda m: gate_up(core, m))
     w_turn(down_w)
@@ -429,6 +489,7 @@
         return copy(st1send, st1recv.at[q], q1s.at[q], q1r.at[q], row_device(q))
 
     pair_row = (1 - yl) * XN + x
+    st1send[...] = jnp.concatenate(lane_sums(stat[0]) * 4, axis=0)
     q1_copy(pair_row).start()
     rs_copy.start()
     for k in range(1, R):
@@ -477,13 +538,18 @@
     h_copy = copy(hbuf.at[yl], hbuf.at[yl], hs, hr, ypair)
     h_arrival = copy(hbuf.at[1 - yl], hbuf.at[1 - yl], hs, hr, ypair)
 
-    def gu_copy(q):
-        part = gubuf.at[my_seat]
-        return copy(part, part, gus.at[q], gur.at[r], row_device(q))
-
-    def gu_arrival(q):
-        part = gubuf.at[seat(q)]
-        return copy(part, part, gus.at[q], gur.at[q], row_device(q))
+    gp_copy = copy(gubuf.at[my_seat], gubuf.at[my_seat], gps, gpr, ypair)
+    pair_seat = x * 2 + 1 - yl
+    gp_arrival = copy(gubuf.at[pair_seat], gubuf.at[pair_seat], gps, gpr, ypair)
+
+    def gu_copy(k):
+        part = gubuf.at[pl.ds(x * 2, 2)]
+        return copy(part, part, gus.at[k], gur.at[k], x_device(x_peer(k)))
+
+    def gu_arrival(k):
+        q = x_peer(XN - k)
+        part = gubuf.at[pl.ds(q * 2, 2)]
+        return copy(part, part, gus.at[k], gur.at[k], x_device(q))
 
     h_copy.start()
     gubuf[my_seat] = total.astype(jnp.bfloat16)
@@ -504,8 +570,7 @@
             oown[m, rows] = dot(act, wdbuf[2 * m + core])
 
     down(yl)
-    for k in range(1, R):
-        gu_copy(row_peer(k)).start()
+    gp_copy.start()
 
     def za_copy(q):
         return copy(
@@ -545,6 +610,9 @@
     h_arrival.wait_recv()
     down(1 - yl)
     pair_sum(1 - yl)
+    gp_arrival.wait_recv()
+    for k in range(1, XN):
+        gu_copy(k).start()
 
     for s in range(2):
         for m in range(YQ):
@@ -606,22 +674,23 @@
         y2_arrival(k).wait_recv()
         yb_copy(k).start()
 
-    output = x_ref[:, 0:F2].astype(jnp.float32)
+    output = xblk[:, 0:F2].astype(jnp.float32)
     for j in range(YH):
         @pl.when(jnp.logical_not(home & (yh == j)))
         def _():
             ya_arrival(j).wait_recv()
         output = output + yra[j].astype(jnp.float32)
     outblk[:, 0:F2] = output.astype(jnp.bfloat16)
-    output = x_ref[:, F2:F].astype(jnp.float32) + zsb[d].astype(jnp.float32)
+    output = xblk[:, F2:F].astype(jnp.float32) + zsb[d].astype(jnp.float32)
     for k in near:
         q = depth_peer(k)
         zb2_arrival(q).wait_recv()
         output = output + zrb[q].astype(jnp.float32)
     outblk[:, F2:F] = output.astype(jnp.bfloat16)
 
-    ga = Gather(outblk, obuf, ozb, a1, a2, a3, a4, a5, a6, a7, a8, a9, a10, a11, a12)
+    ga = Gather(outblk, outblk, obuf, ozb, a1, a2, a3, a4, a5, a6, a7, a8, a9, a10, a11, a12)
     ga.start()
+    ga.keep()
 
     for k in range(1, XN):
         q = x_peer(XN - k)
@@ -652,13 +721,16 @@
         def _():
             q1_arrival(q).wait_recv()
 
+    coef_of(x)
+    coef_of(XN + x)
+
     def coef_step(k):
-        q = row_peer(k)
-        gu_arrival(q).wait_recv()
+        gu_arrival(k).wait_recv()
+        q = x_peer(XN - k)
         coef_of(q)
-
-    loop(R, coef_step, 1)
-    coef_of(r)
+        coef_of(XN + q)
+
+    loop(XN, coef_step, 1)
 
     ga.pass_on(near)
     ga.pass_on_upper()
@@ -670,18 +742,15 @@
 
     def stats(which, m):
         wide = obuf[which, m].reshape(N, F).astype(jnp.float32)
-        head = gvbuf[which, m, 1:2, :]
-        squares = jnp.sum(wide * wide, axis=1, keepdims=True)
-        products = jnp.sum(wide * head, axis=1, keepdims=True)
-        for s in range(2):
-            part = slice(s * L, (s + 1) * L)
-            st2send[s:s + 1, :] += to_lanes(squares[part])
-            st2send[2 + s:3 + s, :] += to_lanes(products[part])
-
-    st2send[...] = jnp.zeros_like(st2send)
+        stat[0] += fold(wide * wide)
+        stat[1] += fold(wide * hdbuf[which, m])
+
+    stat[...] = jnp.zeros_like(stat)
     loop(YQ, lambda m: stats(core, m))
+    hb_arrival.wait_recv()
     ga.arrived()
     loop(YQ, lambda m: stats(1 - core, m))
+    st2send[...] = jnp.concatenate((lane_sums(stat[0]) + lane_sums(stat[1])) * 2, axis=0)
     q2_copy = copy(st2send, st2recv, q2s, q2r, ypair)
     q2_copy.start()
 
@@ -711,7 +780,23 @@
     sums = st2send[...] + st2recv[...]
     inv_final = lax.rsqrt(sums[0:2] / features + norm_eps)
     values = sums[2:4] * inv_final
-    val_ref[...] = jnp.broadcast_to(values[None], (4, 2, L)).reshape(8, L)
+    value_row = jnp.where(place_row == 0, values[0:1], values[1:2])
+    own_values = jnp.sum(
+        jnp.where(
+            lax.broadcasted_iota(jnp.int32, (B, L), 1)
+            == place_lane + lax.broadcasted_iota(jnp.int32, (B, L), 0),
+            value_row, 0.0,
+        ),
+        axis=1, keepdims=True,
+    )
+    val_ref[...] = jnp.sum(
+        jnp.where(
+            lax.broadcasted_iota(jnp.int32, (B, 128), 1)
+            == lax.broadcasted_iota(jnp.int32, (B, 128), 0),
+            own_values, 0.0,
+        ),
+        axis=0, keepdims=True,
+    )
     slope = jnp.clip(values - target[0:2], -huber_delta, huber_delta)
     scale_lanes = inv_final * slope
     shrink_lanes = inv_final * inv_final * (slope * values / features)
@@ -742,7 +827,7 @@
         which = rem(fl, 2)
         m = lax.div(fl, jnp.int32(2))
         wide = obuf[which, m].reshape(N, F).astype(jnp.float32)
-        head = gvbuf[which, m, 1:2, :]
+        head = hdbuf[which, m]
         gobuf[fl] = (scale * head - shrink * wide).astype(jnp.bfloat16)
         gsum[pl.ds(fl, 1), :] = jnp.sum(wide * scale, axis=0, keepdims=True)
         ghpart[...] += dot_t(gobuf[fl], wdbuf[fl])
@@ -781,7 +866,7 @@
     for k in range(1, XN):
         o2_arrival(k).wait_recv()
         o3_copy(k).start()
-    head = gvbuf[rem(x, 2), lax.div(x, jnp.int32(2)), 1:2, :]
+    head = hdbuf[rem(x, 2), lax.div(x, jnp.int32(2))]
     for k in range(1, XN):
         q = x_peer(XN - k)
         sc_arrival(k).wait_recv()
@@ -828,17 +913,17 @@
     for k in range(1, XN):
         head_sum = head_sum + grecv[side * XN + k]
     pick = lax.broadcasted_iota(jnp.int32, head_sum.shape, 0) == c - side * XN
-    gval_ref[...] = jnp.broadcast_to(
-        jnp.sum(jnp.where(pick, head_sum, 0.0), axis=0, keepdims=True), gval_ref.shape
-    )
+    gval_ref[...] = jnp.sum(jnp.where(pick, head_sum, 0.0), axis=0, keepdims=True)
 
     gx.drain()
     ga.drain()
     for j in range(YH):
         @pl.when((yl == 0) & jnp.logical_not(home & (yh == j)))
         def _():
-            gv_copy(j).wait_send()
+            gn_copy(j).wait_send()
+            hd_copy(j).wait_send()
     gb_copy.wait_send()
+    hb_copy.wait_send()
     t1_copy.wait_send()
     rs_copy.wait_send()
     q2_copy.wait_send()
@@ -846,9 +931,11 @@
 
     w_drain(gate_w, up_w, down_w)
     h_copy.wait_send()
+    gp_copy.wait_send()
 
     def x_sends(k):
         y2_copy(k).wait_send()
+        gu_copy(k).wait_send()
         yb_copy(k).wait_send()
         o2_copy(k).wait_send()
         o3_copy(k).wait_send()
@@ -859,7 +946,6 @@
     def row_sends(k):
         q = row_peer(k)
         q1_copy(q).wait_send()
-        gu_copy(q).wait_send()
         gh_copy(q).wait_send()
         gvo_copy(q).wait_send()
 
@@ -880,6 +966,29 @@
                 yb2_copy(s, m).wait_send()
 
 
+def hand_out(
+    dg_ref, du_ref, dd_ref, val_ref, gval_ref,
+    dg_out, du_out, dd_out, val_out, gval_out,
+    dg_buf, du_buf, dd_buf, fetched, stored,
+):
+    parts = ((dg_ref, dg_buf, dg_out), (du_ref, du_buf, du_out), (dd_ref, dd_buf, dd_out))
+    reads = [
+        pltpu.make_async_copy(src, buf, fetched.at[i]) for i, (src, buf, _) in enumerate(parts)
+    ]
+    writes = [
+        pltpu.make_async_copy(buf, dst, stored.at[i]) for i, (_, buf, dst) in enumerate(parts)
+    ]
+    for one in reads:
+        one.start()
+    val_out[...] = val_ref[:, 0:val_out.shape[1]]
+    gval_out[...] = gval_ref[...]
+    for read, write in zip(reads, writes):
+        read.wait()
+        write.start()
+    for one in writes:
+        one.wait()
+
+
 def build(mesh):
     R, C, Z = mesh.shape["row"], mesh.shape["col"], mesh.shape["depth"]
     YH, XN = C // 2, R // 2
@@ -890,14 +999,7 @@
         H = w_gate.shape[1]
         N = Z * 2 * B
         L = N // 2
-        r = lax.axis_index("row")
-        d = lax.axis_index("depth")
-        place = d * (2 * B) + (r // XN) * B
-        target = jnp.take(return_table, sample_index)
-        tile = lax.dynamic_update_slice(
-            jnp.zeros((8, L), jnp.float32), target[None, :], (place // L, place % L)
-        )
-        gv = jnp.zeros((8, F), jnp.float32).at[0].set(pre_gain).at[1].set(value_head)
+        entries = return_table.shape[0]
 
         bf, f32 = jnp.bfloat16, jnp.float32
         V = pltpu.VMEM
@@ -911,8 +1013,10 @@
             V((2, YQ, Z, 2, B, F), bf), V((Z, B, F2), bf),
             V((XN, N, F), bf), V((XN, N, F), bf), V((F, XN * N), bf),
             V((XN, F, H), bf), V((XN, F, H), bf), V((XN, H, F), bf),
-            V((2, YQ, 8, F), f32), V((8, L), f32), V((8, L), f32), V((Z, 8, L), f32),
-            V((N, 2 * H), f32), V((L, 2 * H), bf), V((L, 2 * H), bf),
+            V((2, YQ, 1, F), f32), V((2, YQ, 1, F), f32), V((B, F), bf),
+            pltpu.SMEM((1, B), jnp.int32), V((entries // 128, 128), f32),
+            V((8, L), f32), V((8, L), f32), V((8, L), f32), V((Z, 8, L), f32),
+            V((N, 2 * H), f32), V((2, N, 128), f32), V((L, 2 * H), bf), V((L, 2 * H), bf),
             V((8, L), f32), V((R, 8, L), f32),
             V((2, L, H), bf), V((H, R * L), bf), V((R, L, 2 * H), bf), V((R, L, 2 * H), f32),
             V((YQ, N, F), bf), V((YQ, N, F), bf), V((YQ, N, F), f32),
@@ -924,10 +1028,10 @@
             V((N, H), f32), V((L, H), bf), V((L, H), bf),
             V((R, L, H), bf), V((R, L, 2 * H), bf), V((8, F), f32), V((R, 8, F), f32),
             *gather,
-            dma(YH), dma(YQ), dma(), dma(), dma(), dma(), dma(Z), dma(Z),
+            dma(YH), dma(YQ), dma(YH), dma(YQ), dma(2), dma(2), dma(5), dma(), dma(), dma(Z), dma(Z),
             dma(3), dma(4), dma(4), dma(4), dma(4), dma(4), dma(4),
             dma(R), dma(R), dma(), dma(), dma(XN), dma(XN), dma(XN), dma(XN),
-            dma(), dma(), dma(R), dma(R),
+            dma(), dma(), dma(), dma(), dma(XN), dma(XN),
             dma(2), dma(2), dma(Z), dma(Z), dma(2 * YQ), dma(YH), dma(2 * YQ), dma(YH),
             dma(Z), dma(Z),
             *gather,
@@ -942,18 +1046,34 @@
                 jax.ShapeDtypeStruct((F, H), bf),
                 jax.ShapeDtypeStruct((F, H), bf),
                 jax.ShapeDtypeStruct((H, F), bf),
-                jax.ShapeDtypeStruct((8, L), f32),
-                jax.ShapeDtypeStruct((8, F), f32),
+                jax.ShapeDtypeStruct((1, 128), f32),
+                jax.ShapeDtypeStruct((1, F), f32),
             ),
-            in_specs=[vmem, vmem, vmem, hbm, hbm, hbm],
+            in_specs=[hbm] * 8,
             out_specs=(vmem,) * 5,
             scratch_shapes=scratch,
             compiler_params=pltpu.CompilerParams(
-                collective_id=0, has_side_effects=True, vmem_limit_bytes=40 * 1024 * 1024
+                collective_id=0, has_side_effects=True, vmem_limit_bytes=VMEM_MB * 1024 * 1024
             ),
-        )(residual, gv, tile, w_gate, w_up, w_down)
-        values = lax.dynamic_slice(values, (place // L, place % L), (1, B))[0]
-        return values, dg, du, dd, gval[0]
+        )(
+            residual, pre_gain.reshape(1, F), value_head.reshape(1, F),
+            sample_index.reshape(1, B), return_table.reshape(entries // 128, 128),
+            w_gate, w_up, w_down,
+        )
+        dg, du, dd, values, gval = pl.pallas_call(
+            hand_out,
+            out_shape=(
+                jax.ShapeDtypeStruct((F, H), bf),
+                jax.ShapeDtypeStruct((F, H), bf),
+                jax.ShapeDtypeStruct((H, F), bf),
+                jax.ShapeDtypeStruct((1, B), f32),
+                jax.ShapeDtypeStruct((1, F), f32),
+            ),
+            in_specs=[hbm, hbm, hbm, vmem, vmem],
+            out_specs=(hbm, hbm, hbm, vmem, vmem),
+            scratch_shapes=[V((F, H), bf), V((F, H), bf), V((H, F), bf), dma(3), dma(3)],
+        )(dg, du, dd, values, gval)
+        return values.reshape(B), dg, du, dd, gval.reshape(F)
 
     return per_device
 

time: 115 us -> 105 us (0.913)
  local copies, waits for them, and re-layouts: 6.61 us -> 0 us
  Pallas kernels: 107 us -> 104 us
    pallas_call x1, Pallas kernels: 107 us -> 101 us  [per_device(): pl.pallas_call(functools.partial(kernel, R, YH, Z, B, F, H), out_shape=(j...]
    unnamed x19 -> x0, local copies, waits for them, and re-layouts: 4.56 us -> none
    pallas_call x0 -> x1, Pallas kernels: none -> 3.13 us  [per_device(): pl.pallas_call(hand_out, out_shape=(jax.ShapeDtypeStruct((F, H), bf), jax...]
where the time goes in v4:
time: 105 us
  Pallas kernels  104 us (99%)
    pallas_call x1, Pallas kernels, per_device(): pl.pallas_call(functools.partial(kernel, R, YH, Z, B, F, H), out_shape=(j...  101 us
    pallas_call x1, Pallas kernels, per_device(): pl.pallas_call(hand_out, out_shape=(jax.ShapeDtypeStruct((F, H), bf), jax...  3.13 us

profile of v4, /device:TPU:1, one launch (start us, length us, event | category | flops | bytes accessed | tf_op | source)
XLA Modules:
  0.0 104.7 jit_solution(16312209645795997915)
XLA Ops:
  0.6 101.0 %shard_map.119 = (bf16[512,256]{1,0:T(8,128)(2,1)}, bf16[512,256]{1,0:T(8,128)(2,1)}, bf16[256,512]{1,0:T(8,128)(2,1)}, f32[1,128]{1,0:T(1,128)}, f32[1,512]{1,0:T(1,128)}) custom-call(bf16[16,512]{1,0:T(8,128)(2,1)} %x_ref.1, f32[1,512]{1,0:T(1,128)} %bitcast.7, f32[1,512]{1,0:T(1,128)} %bitcast.8, s32[1,16]{1,0:T(1,128)} %bitcast.9, f32[256,128]{1,0:T(8,128)} %bitcast.6, ...), custom_call_target="tpu_custom_call" | custom-call | tf_op jit(solution)/shard_map/pallas_call | solution.py:1043
  101.6 3.1 %shard_map.120 = (bf16[512,256]{1,0:T(8,128)(2,1)}, bf16[512,256]{1,0:T(8,128)(2,1)}, bf16[256,512]{1,0:T(8,128)(2,1)}, f32[1,16]{1,0:T(1,128)}, f32[1,512]{1,0:T(1,128)}) custom-call(bf16[512,256]{1,0:T(8,128)(2,1)} %get-tuple-element.15.dg_ref, bf16[512,256]{1,0:T(8,128)(2,1)} %get-tuple-element.16.du_ref, bf16[256,512]{1,0:T(8,128)(2,1)} %get-tuple-element.17.dd_ref, ...), custom_call_target="tpu_custom_call" | custom-call | tf_op jit(solution)/shard_map/pallas_call | solution.py:1063

commit v5 on v4

--- a/solution.py
+++ b/solution.py
@@ -336,22 +336,31 @@
     for one in local_weights():
         one.start()
 
-    def w_copy(ref, buf, send, recv, k):
-        return copy(ref, buf.at[x], send.at[k], recv.at[k], x_device(x_peer(k)))
-
-    def w_arrival(ref, buf, send, recv, k):
+    def half_rows(ref, k, i):
+        rows = ref.shape[0] // 2
+        return pl.ds(rows * ((0 if k == 1 else 1) ^ i), rows)
+
+    def w_copy(ref, buf, send, recv, k, i):
+        rows = half_rows(ref, k, i)
+        return copy(
+            ref.at[rows], buf.at[x, rows], send.at[2 * k + i], recv.at[2 * k + i],
+            x_device(x_peer(k)),
+        )
+
+    def w_arrival(ref, buf, send, recv, k, i):
         q = x_peer(XN - k)
-        return copy(ref, buf.at[q], send.at[k], recv.at[k], x_device(q))
+        rows = half_rows(ref, k, i)
+        return copy(
+            ref.at[rows], buf.at[q, rows], send.at[2 * k + i], recv.at[2 * k + i], x_device(q)
+        )
 
     def w_onward(ref, buf, send, recv, k):
-        rows = ref.shape[0] // 2
-        part = buf.at[x_peer(XN - k), pl.ds(0 if k == 1 else rows, rows)]
-        return copy(part, part, send.at[k - 1], recv.at[k - 1], x_device(x_peer(k)))
+        part = buf.at[x_peer(XN - k), half_rows(ref, k, 0)]
+        return copy(part, part, send.at[2 * (k - 1)], recv.at[2 * (k - 1)], x_device(x_peer(k)))
 
     def w_onward_arrival(ref, buf, send, recv, k):
-        rows = ref.shape[0] // 2
-        part = buf.at[x_peer(2), pl.ds(0 if k == 1 else rows, rows)]
-        return copy(part, part, send.at[k - 1], recv.at[k - 1], x_device(x_peer(XN - k)))
+        part = buf.at[x_peer(2), half_rows(ref, k, 0)]
+        return copy(part, part, send.at[2 * (k - 1)], recv.at[2 * (k - 1)], x_device(x_peer(XN - k)))
 
     gate_w = (wg_ref, wgbuf, wgs, wgr)
     up_w = (wu_ref, wubuf, wus, wur)
@@ -359,18 +368,22 @@
     sides = (1,) if XN == 2 else (1, 3)
 
     def w_start(*which):
-        for k in sides:
-            for w in which:
-                w_copy(*w, k).start()
+        for i in range(2):
+            for k in sides:
+                for w in which:
+                    w_copy(*w, k, i).start()
 
     def w_turn(*which):
         for k in sides:
             for w in which:
-                w_arrival(*w, k).wait_recv()
+                w_arrival(*w, k, 0).wait_recv()
                 if XN == 4:
                     w_onward(*w, k).start()
 
     def w_finish(*which):
+        for k in sides:
+            for w in which:
+                w_arrival(*w, k, 1).wait_recv()
         if XN == 4:
             for k in sides:
                 for w in which:
@@ -379,7 +392,8 @@
     def w_drain(*which):
         for k in sides:
             for w in which:
-                w_copy(*w, k).wait_send()
+                w_copy(*w, k, 0).wait_send()
+                w_copy(*w, k, 1).wait_send()
                 if XN == 4:
                     w_onward(*w, k).wait_send()
 
@@ -791,8 +805,8 @@
     )
     val_ref[...] = jnp.sum(
         jnp.where(
-            lax.broadcasted_iota(jnp.int32, (B, 128), 1)
-            == lax.broadcasted_iota(jnp.int32, (B, 128), 0),
+            lax.broadcasted_iota(jnp.int32, (B, B), 1)
+            == lax.broadcasted_iota(jnp.int32, (B, B), 0),
             own_values, 0.0,
         ),
         axis=0, keepdims=True,
@@ -966,22 +980,19 @@
                 yb2_copy(s, m).wait_send()
 
 
-def hand_out(
-    dg_ref, du_ref, dd_ref, val_ref, gval_ref,
-    dg_out, du_out, dd_out, val_out, gval_out,
-    dg_buf, du_buf, dd_buf, fetched, stored,
-):
-    parts = ((dg_ref, dg_buf, dg_out), (du_ref, du_buf, du_out), (dd_ref, dd_buf, dd_out))
+def hand_out(*refs):
+    sources, targets, buffers = refs[0:5], refs[5:10], refs[10:15]
+    fetched, stored = refs[15:]
     reads = [
-        pltpu.make_async_copy(src, buf, fetched.at[i]) for i, (src, buf, _) in enumerate(parts)
+        pltpu.make_async_copy(src, buf, fetched.at[i])
+        for i, (src, buf) in enumerate(zip(sources, buffers))
     ]
     writes = [
-        pltpu.make_async_copy(buf, dst, stored.at[i]) for i, (_, buf, dst) in enumerate(parts)
+        pltpu.make_async_copy(buf, dst, stored.at[i])
+        for i, (buf, dst) in enumerate(zip(buffers, targets))
     ]
     for one in reads:
         one.start()
-    val_out[...] = val_ref[:, 0:val_out.shape[1]]
-    gval_out[...] = gval_ref[...]
     for read, write in zip(reads, writes):
         read.wait()
         write.start()
@@ -1029,7 +1040,7 @@
             V((R, L, H), bf), V((R, L, 2 * H), bf), V((8, F), f32), V((R, 8, F), f32),
             *gather,
             dma(YH), dma(YQ), dma(YH), dma(YQ), dma(2), dma(2), dma(5), dma(), dma(), dma(Z), dma(Z),
-            dma(3), dma(4), dma(4), dma(4), dma(4), dma(4), dma(4),
+            dma(3), dma(8), dma(8), dma(8), dma(8), dma(8), dma(8),
             dma(R), dma(R), dma(), dma(), dma(XN), dma(XN), dma(XN), dma(XN),
             dma(), dma(), dma(), dma(), dma(XN), dma(XN),
             dma(2), dma(2), dma(Z), dma(Z), dma(2 * YQ), dma(YH), dma(2 * YQ), dma(YH),
@@ -1046,7 +1057,7 @@
                 jax.ShapeDtypeStruct((F, H), bf),
                 jax.ShapeDtypeStruct((F, H), bf),
                 jax.ShapeDtypeStruct((H, F), bf),
-                jax.ShapeDtypeStruct((1, 128), f32),
+                jax.ShapeDtypeStruct((1, B), f32),
                 jax.ShapeDtypeStruct((1, F), f32),
             ),
             in_specs=[hbm] * 8,
@@ -1069,9 +1080,12 @@
                 jax.ShapeDtypeStruct((1, B), f32),
                 jax.ShapeDtypeStruct((1, F), f32),
             ),
-            in_specs=[hbm, hbm, hbm, vmem, vmem],
-            out_specs=(hbm, hbm, hbm, vmem, vmem),
-            scratch_shapes=[V((F, H), bf), V((F, H), bf), V((H, F), bf), dma(3), dma(3)],
+            in_specs=[hbm] * 5,
+            out_specs=(hbm,) * 5,
+            scratch_shapes=[
+                V((F, H), bf), V((F, H), bf), V((H, F), bf), V((1, B), f32), V((1, F), f32),
+                dma(5), dma(5),
+            ],
         )(dg, du, dd, values, gval)
         return values.reshape(B), dg, du, dd, gval.reshape(F)
 

time: 105 us -> 102 us (0.971); the launches traced: 105 us -> 100 us
  Pallas kernels: 104 us -> 99.4 us
    pallas_call x1, Pallas kernels: 101 us -> 97.5 us  [per_device(): pl.pallas_call(functools.partial(kernel, R, YH, Z, B, F, H), out_shape=(j...]
    pallas_call x1, Pallas kernels: 3.13 us -> 1.92 us  [per_device(): pl.pallas_call(hand_out, out_shape=(jax.ShapeDtypeStruct((F, H), bf), jax...]
where the time goes in v5:
time: 102 us; the launch traced here: 100 us
  Pallas kernels  99.4 us (97%)
    pallas_call x1, Pallas kernels, per_device(): pl.pallas_call(functools.partial(kernel, R, YH, Z, B, F, H), out_shape=(j...  97.5 us

profile of v5, /device:TPU:1, one launch (start us, length us, event | category | flops | bytes accessed | tf_op | source)
XLA Modules:
  0.0 100.0 jit_solution(6822000975187777437)
XLA Ops:
  0.6 97.5 %shard_map.119 = (bf16[512,256]{1,0:T(8,128)(2,1)}, bf16[512,256]{1,0:T(8,128)(2,1)}, bf16[256,512]{1,0:T(8,128)(2,1)}, f32[1,16]{1,0:T(1,128)}, f32[1,512]{1,0:T(1,128)}) custom-call(bf16[16,512]{1,0:T(8,128)(2,1)} %x_ref.1, f32[1,512]{1,0:T(1,128)} %bitcast.7, f32[1,512]{1,0:T(1,128)} %bitcast.8, s32[1,16]{1,0:T(1,128)} %bitcast.9, f32[256,128]{1,0:T(8,128)} %bitcast.6, ...), custom_call_target="tpu_custom_call" | custom-call | tf_op jit(solution)/shard_map/pallas_call | solution.py:1054
  98.1 1.9 %shard_map.120 = (bf16[512,256]{1,0:T(8,128)(2,1)}, bf16[512,256]{1,0:T(8,128)(2,1)}, bf16[256,512]{1,0:T(8,128)(2,1)}, f32[1,16]{1,0:T(1,128)}, f32[1,512]{1,0:T(1,128)}) custom-call(bf16[512,256]{1,0:T(8,128)(2,1)} %get-tuple-element.15.refs_0_, bf16[512,256]{1,0:T(8,128)(2,1)} %get-tuple-element.16.refs_1_, bf16[256,512]{1,0:T(8,128)(2,1)} %get-tuple-element.17.refs_2_, ...), custom_call_target="tpu_custom_call" | custom-call | tf_op jit(solution)/shard_map/pallas_call | solution.py:1074
